TPU v7x, 512 devices: a whole 4x8x8 slice. The times are simulated.
512 devices in a mesh: blk: 128 (over x, y_lo, z), rep: 4 (over y_hi, core).
Axes of the slice: x: 4, y: 8 (y_hi: 2, y_lo: 4; y = y_hi * 4 + y_lo), z: 8, core: 2. Of those that a mesh axis runs over, the one named last changes fastest.
Arguments:
- positions: float32 [3, 262144], P(None, ('blk', 'rep')), may hold values from -6 to 6
- normal_flow: float32 [3, 262144], P(None, ('blk', 'rep')), may hold values from -6 to 6
- send_owner: int32 [262144], P(('blk', 'rep')), may hold values from 0 to 127, as said below
- send_slot: int32 [262144], P(('blk', 'rep')), may hold values from 0 to 9, as said below
- recv_index: int32 [655360], P(('blk', 'rep')), may hold values from -1 to 1279, as said below
- loop_pos: int32 [655360], P(('blk', 'rep')), may hold values from 0 to 1279, as said below
- loop_len: int32 [655360], P(('blk', 'rep')), may hold values from 1 to 1280, as said below
Outputs:
- velocity: float32 [3, 262144], P(None, ('blk', 'rep'))
Inputs may be any that keep to these rules, and one draw needn't show every extreme that they name: `send_slot`: A filament's points all lie on devices with one rep index, and its owner device has that rep index. No two points of one device share an owner and slot; at most 10 points go from one device to one owner, and some pair reaches it. `send_owner`: owner blk indices. `recv_index`: for each owner device, entry b * 10 + s is the owner-local column of the point arriving from the device of blk index b in slot s, or -1 where no point arrives; every point has its entry and no column is named twice. One owner holds up to 1280 points, and some owner holds that many. `loop_pos`: the owner-local points of one filament are consecutive columns of one device in filament order; unused columns have order 0. Some filament has 1280 points. `loop_len`: every filament has 16 or more points and at most 1280, a count reached by some filament; unused owner-local columns have 1.
All inputs are finite; a program needn't handle non-finite values.
Results may differ from a plain program's by a relative error of at most 0.0003.
Values sent between devices are 32-bit elements; how exact they have to be, the bound alone decides.
A program may use at most 64 MiB of HBM per device.

v0:
```python
import jax
import jax.numpy as jnp
from jax import lax
from jax.sharding import PartitionSpec as P

STOPS = 8


LOCAL_BETA = 0.3
FRICTION_ALPHA = 0.21
FRICTION_PRIME = 0.06
BIOT_SCALE = 0.01
CORE_SQUARED = 0.25
SPEED_FLOOR = 1.0


def passed_along(value, axis, steps):
    count = lax.axis_size(axis)
    pairs = [(source, (source + steps) % count) for source in range(count)]
    return lax.ppermute(value, axis, pairs)


def cross_product(left, right):
    return jnp.stack(
        [
            left[1] * right[2] - left[2] * right[1],
            left[2] * right[0] - left[0] * right[2],
            left[0] * right[1] - left[1] * right[0],
        ]
    )


def induced(targets, sources, tangents):
    total_targets = targets.shape[1]
    block_width = min(256, total_targets)
    blocks = targets.reshape(3, total_targets // block_width, block_width).transpose(1, 0, 2)

    def one_block(target_block):
        separation = target_block[:, :, None] - sources[:, None, :]
        radius_sq = jnp.sum(separation * separation, axis=0) + CORE_SQUARED
        weight = 1.0 / (radius_sq * jnp.sqrt(radius_sq))
        turned = cross_product(tangents[:, None, :], separation)
        return jnp.sum(turned * weight[None], axis=2)

    return lax.map(one_block, blocks).transpose(1, 0, 2).reshape(3, total_targets)


def along_loops(owned, loop_pos, loop_len):
    point_index = jnp.arange(owned.shape[1], dtype=jnp.int32)
    loop_start = point_index - loop_pos

    def neighbour(offset):
        return jnp.take(owned, loop_start + jnp.remainder(loop_pos + offset, loop_len), axis=1)

    plus_one, minus_one = (neighbour(1), neighbour(-1))
    plus_two, minus_two = (neighbour(2), neighbour(-2))
    first_derivative = (8.0 * (plus_one - minus_one) - (plus_two - minus_two)) / 12.0
    second_derivative = (
        16.0 * (plus_one + minus_one) - (plus_two + minus_two) - 30.0 * owned
    ) / 12.0
    return (first_derivative, second_derivative)


def shards(positions, normal_flow, send_owner, send_slot, recv_index, loop_pos, loop_len):
    owners = lax.axis_size("blk")
    point_count = positions.shape[1]
    capacity = recv_index.shape[0] // owners
    owner_capacity = loop_pos.shape[0]
    send_column = send_owner * capacity + send_slot
    outgoing = jnp.zeros((3, owners * capacity), jnp.float32).at[:, send_column].set(positions)
    arrived = lax.all_to_all(
        outgoing.reshape(3, owners, capacity), "blk", split_axis=1, concat_axis=1, tiled=True
    )
    arrived = arrived.reshape(3, owners * capacity)
    target_slot = jnp.where(recv_index >= 0, recv_index, owner_capacity)
    owned = (
        jnp.zeros((3, owner_capacity + 1), jnp.float32)
        .at[:, target_slot]
        .set(arrived)[:, :owner_capacity]
    )
    first_derivative, second_derivative = along_loops(owned, loop_pos, loop_len)
    derivatives = jnp.concatenate([first_derivative, second_derivative], axis=0)
    leaving = jnp.take(derivatives, jnp.maximum(recv_index, 0), axis=1)
    returned = lax.all_to_all(
        leaving.reshape(6, owners, capacity), "blk", split_axis=1, concat_axis=1, tiled=True
    )
    received_back = jnp.take(returned.reshape(6, owners * capacity), send_column, axis=1)
    tangent = received_back[:3]
    curvature = received_back[3:]
    speed_squared = jnp.maximum(jnp.sum(tangent * tangent, axis=0), SPEED_FLOOR)
    local_term = (
        LOCAL_BETA * cross_product(tangent, curvature) / (speed_squared * jnp.sqrt(speed_squared))
    )
    replica_index = lax.axis_index("rep")
    stacked = jnp.concatenate([positions, tangent], axis=0)
    targets = lax.all_gather(positions, "rep", axis=1, tiled=True)

    def contribution(carried):
        return induced(targets, carried[:3], carried[3:])

    far_total = contribution(stacked)
    shift_steps = [-1] * (STOPS // 2) + [STOPS // 2 + 1] + [1] * (STOPS // 2 - 2)
    carried = stacked
    for step_size in shift_steps:
        carried = passed_along(carried, "blk", step_size)
        far_total = far_total + contribution(carried)
    summed_group = lax.psum(far_total, "rep")
    far_sum = lax.dynamic_slice_in_dim(summed_group, replica_index * point_count, point_count, 1)
    superfluid = local_term + BIOT_SCALE * far_sum
    unit_tangent = tangent / jnp.sqrt(speed_squared)
    slip_velocity = normal_flow - superfluid
    first_turn = cross_product(unit_tangent, slip_velocity)
    return (
        superfluid
        + FRICTION_ALPHA * first_turn
        - FRICTION_PRIME * cross_product(unit_tangent, first_turn)
    )


def solution(mesh):
    return jax.shard_map(
        shards,
        mesh=mesh,
        in_specs=(
            P(None, ("blk", "rep")),
            P(None, ("blk", "rep")),
            P(("blk", "rep")),
            P(("blk", "rep")),
            P(("blk", "rep")),
            P(("blk", "rep")),
            P(("blk", "rep")),
        ),
        out_specs=P(None, ("blk", "rep")),
        check_vma=False,
    )
```

profile of v0, /device:TPU:1, one launch (start us, length us, event | category | flops | bytes accessed | tf_op | source)
XLA Modules:
  0.0 201.0 jit_solution(12040956339280715440)
XLA Ops:
  0.0 0.9 copy.147
  1.6 1.9 scatter_custom_fusion
  3.9 0.8 copy.149
  4.8 18.6 %all-to-all-start = ((f32[3,128,10]{2,0,1:T(4,128)}), f32[3,128,10]{2,0,1:T(4,128)S(1)}, u32[]{:S(2)}, u32[]{:S(2)}) async-start(f32[3,128,10]{2,0,1:T(4,128)} %copy.149), calls=%async_computation | async-start | bytes 524288 | tf_op jit(solution)/shard_map/all_to_all | solution.py:71
  24.0 9.9 %all_gather.3 = f32[3,2048]{1,0:T(4,128)S(1)} all-gather(f32[3,512]{1,0:T(4,128)S(1)} %copy-done), channel_id=1, replica_groups=mesh['blk'=128,'rep'=4] {'rep'}, dimensions={1}, use_global_device_ids=true | all-gather | bytes 30720 | tf_op jit(solution)/shard_map/all_gather | solution.py:96
  33.9 2.5 %all-to-all-done = f32[3,128,10]{2,0,1:T(4,128)S(1)} async-done(((f32[3,128,10]{2,0,1:T(4,128)}), f32[3,128,10]{2,0,1:T(4,128)S(1)}, u32[]{:S(2)}, u32[]{:S(2)}) %all-to-all-start) | async-done | bytes 15392 | tf_op jit(solution)/shard_map/all_to_all | solution.py:71
  36.9 6.3 %scatter_custom_fusion.1 = f32[3,1281]{0,1:T(8,128)S(1)} fusion(s32[1280]{0:T(1024)S(1)} %get-tuple-element.509, f32[1280,3]{1,0:T(8,128)S(1)} %copy.151, f32[]{:T(128)} %constant.187.clone.1), kind=kCustom, calls=%fused_computation.96 | custom fusion | bytes 15376 | tf_op jit(solution)/shard_map/scatter | solution.py:79
  43.4 2.4 %gather_fusion.2 = f32[1280,3]{1,0:T(8,128)S(1)} fusion(f32[3,1280]{0,1:T(8,128)S(1)} %slice.389, s32[2048]{0:T(1024)S(1)} %get-tuple-element.515), kind=kCustom, calls=%fused_computation.clone | custom fusion | bytes 35840 | tf_op jit(solution)/shard_map/jit(_take)/gather | solution.py:53
  46.0 2.4 %gather_fusion.3 = f32[1280,3]{1,0:T(8,128)S(1)} fusion(f32[3,1280]{0,1:T(8,128)S(1)} %slice.389, s32[2048]{0:T(1024)S(1)} %get-tuple-element.514), kind=kCustom, calls=%fused_computation.1.clone | custom fusion | bytes 35840 | tf_op jit(solution)/shard_map/jit(_take)/gather | solution.py:53
  48.6 2.4 %gather_fusion.4 = f32[1280,3]{1,0:T(8,128)S(1)} fusion(f32[3,1280]{0,1:T(8,128)S(1)} %slice.389, s32[2048]{0:T(1024)S(1)} %get-tuple-element.513), kind=kCustom, calls=%fused_computation.2.clone | custom fusion | bytes 35840 | tf_op jit(solution)/shard_map/jit(_take)/gather | solution.py:53
  51.2 2.4 %gather_fusion.5 = f32[1280,3]{1,0:T(8,128)S(1)} fusion(f32[3,1280]{0,1:T(8,128)S(1)} %slice.389, s32[2048]{0:T(1024)S(1)} %get-tuple-element.512), kind=kCustom, calls=%fused_computation.3.clone | custom fusion | bytes 35840 | tf_op jit(solution)/shard_map/jit(_take)/gather | solution.py:53
  54.1 2.4 %gather_fusion = f32[1280,6]{1,0:T(8,128)S(1)} fusion(f32[6,1280]{0,1:T(8,128)S(1)} %copy.161, s32[2048]{0:T(1024)S(1)} %pad_clamp_fusion), kind=kCustom, calls=%fused_computation.4 | custom fusion | bytes 66560 | tf_op jit(solution)/shard_map/jit(_take)/gather | solution.py:83
  57.1 1.0 copy.163
  58.1 11.5 %all-to-all-start.1 = ((f32[6,128,10]{2,0,1:T(8,128)}), f32[6,128,10]{2,0,1:T(8,128)S(1)}, u32[]{:S(2)}, u32[]{:S(2)}) async-start(f32[6,128,10]{2,0,1:T(8,128)} %copy.163), calls=%async_computation.1 | async-start | bytes 1048576 | tf_op jit(solution)/shard_map/all_to_all | solution.py:84
  69.7 18.1 %all-to-all-done.1 = f32[6,128,10]{2,0,1:T(8,128)S(1)} async-done(((f32[6,128,10]{2,0,1:T(8,128)}), f32[6,128,10]{2,0,1:T(8,128)S(1)}, u32[]{:S(2)}, u32[]{:S(2)}) %all-to-all-start.1) | async-done | bytes 30752 | tf_op jit(solution)/shard_map/all_to_all | solution.py:84
  88.3 1.0 gather_fusion.1
  89.6 5.5 %collective-permute-start = (f32[6,512]{1,0:T(8,128)S(1)}, f32[6,512]{1,0:T(8,128)S(1)}, u32[]{:S(2)}, u32[]{:S(2)}) collective-permute-start(f32[6,512]{1,0:T(8,128)S(1)} %pad_maximum_fusion.1), channel_id=1, source_target_pairs={{0,508},{4,0},{8,4},{12,8},{16,12},{20,16},{24,20},{28,24},{32,28}... | collective-permute-start | bytes 36872 | tf_op jit(solution)/shard_map/ppermute | solution.py:20
  95.1 8.1 %while.80 = (s32[]{:T(128)}, f32[8,3,256]{2,1,0:T(4,128)S(1)}, f32[3,512]{1,0:T(4,128)S(1)}, f32[8,3,256]{2,1,0:T(4,128)S(1)}, f32[3,512]{1,0:T(4,128)S(1)}, /*index=5*/s32[]{:T(128)}) while((s32[]{:T(128)}, f32[8,3,256]{2,1,0:T(4,128)S(1)}, f32[3,512]{1,0:T(4,128)S(1)}, f32[8,3,256]{2,1,0:T(4,128)S(1)}, f32[3,512]{1,0:T(4,128)S(1)}, ...), condition=%wide.region_6.8_spmd, body=%wide.region_3.7_spmd.sunk | while | flops 4193538 | bytes 8433741 | solution.py:45
  103.2 2.4 %collective-permute-start.1 = (f32[6,512]{1,0:T(8,128)S(1)}, f32[6,512]{1,0:T(8,128)S(1)}, u32[]{:S(2)}, u32[]{:S(2)}) collective-permute-start(f32[6,512]{1,0:T(8,128)S(1)} %collective-permute-done), channel_id=1, source_target_pairs={{0,508},{4,0},{8,4},{12,8},{16,12},{20,16},{24,20},{28,24},{32,28}... | collective-permute-start | bytes 36872 | tf_op jit(solution)/shard_map/ppermute | solution.py:20
  105.5 8.1 %while.81 = (s32[]{:T(128)}, f32[8,3,256]{2,1,0:T(4,128)S(1)}, f32[3,512]{1,0:T(4,128)S(1)}, f32[8,3,256]{2,1,0:T(4,128)S(1)}, f32[3,512]{1,0:T(4,128)S(1)}, /*index=5*/s32[]{:T(128)}) while((s32[]{:T(128)}, f32[8,3,256]{2,1,0:T(4,128)S(1)}, f32[3,512]{1,0:T(4,128)S(1)}, f32[8,3,256]{2,1,0:T(4,128)S(1)}, f32[3,512]{1,0:T(4,128)S(1)}, ...), condition=%wide.region_10.12_spmd, body=%wide.region_7.11_spmd.sunk | while | flops 4193538 | bytes 8433741 | solution.py:45
  113.6 2.4 %collective-permute-start.2 = (f32[6,512]{1,0:T(8,128)S(1)}, f32[6,512]{1,0:T(8,128)S(1)}, u32[]{:S(2)}, u32[]{:S(2)}) collective-permute-start(f32[6,512]{1,0:T(8,128)S(1)} %collective-permute-done.1), channel_id=1, source_target_pairs={{0,508},{4,0},{8,4},{12,8},{16,12},{20,16},{24,20},{28,24},{32,28}... | collective-permute-start | bytes 36872 | tf_op jit(solution)/shard_map/ppermute | solution.py:20
  116.0 8.1 %while.82 = (s32[]{:T(128)}, f32[8,3,256]{2,1,0:T(4,128)S(1)}, f32[3,512]{1,0:T(4,128)S(1)}, f32[8,3,256]{2,1,0:T(4,128)S(1)}, f32[3,512]{1,0:T(4,128)S(1)}, /*index=5*/s32[]{:T(128)}) while((s32[]{:T(128)}, f32[8,3,256]{2,1,0:T(4,128)S(1)}, f32[3,512]{1,0:T(4,128)S(1)}, f32[8,3,256]{2,1,0:T(4,128)S(1)}, f32[3,512]{1,0:T(4,128)S(1)}, ...), condition=%wide.region_14.16_spmd, body=%wide.region_11.15_spmd.sunk | while | flops 4193538 | bytes 8433741 | solution.py:45
  124.1 2.4 %collective-permute-start.3 = (f32[6,512]{1,0:T(8,128)S(1)}, f32[6,512]{1,0:T(8,128)S(1)}, u32[]{:S(2)}, u32[]{:S(2)}) collective-permute-start(f32[6,512]{1,0:T(8,128)S(1)} %collective-permute-done.2), channel_id=1, source_target_pairs={{0,508},{4,0},{8,4},{12,8},{16,12},{20,16},{24,20},{28,24},{32,28}... | collective-permute-start | bytes 36872 | tf_op jit(solution)/shard_map/ppermute | solution.py:20
  126.5 8.1 %while.83 = (s32[]{:T(128)}, f32[8,3,256]{2,1,0:T(4,128)S(1)}, f32[3,512]{1,0:T(4,128)S(1)}, f32[8,3,256]{2,1,0:T(4,128)S(1)}, f32[3,512]{1,0:T(4,128)S(1)}, /*index=5*/s32[]{:T(128)}) while((s32[]{:T(128)}, f32[8,3,256]{2,1,0:T(4,128)S(1)}, f32[3,512]{1,0:T(4,128)S(1)}, f32[8,3,256]{2,1,0:T(4,128)S(1)}, f32[3,512]{1,0:T(4,128)S(1)}, ...), condition=%wide.region_18.20_spmd, body=%wide.region_15.19_spmd.sunk | while | flops 4193538 | bytes 8433741 | solution.py:45
  134.6 2.3 %collective-permute-start.4 = (f32[6,512]{1,0:T(8,128)S(1)}, f32[6,512]{1,0:T(8,128)S(1)}, u32[]{:S(2)}, u32[]{:S(2)}) collective-permute-start(f32[6,512]{1,0:T(8,128)S(1)} %collective-permute-done.3), channel_id=1, source_target_pairs={{0,20},{4,24},{8,28},{12,32},{16,36},{20,40},{24,44},{28,48},{32,5... | collective-permute-start | bytes 36872 | tf_op jit(solution)/shard_map/ppermute | solution.py:20
  136.9 8.1 %while.84 = (s32[]{:T(128)}, f32[8,3,256]{2,1,0:T(4,128)S(1)}, f32[3,512]{1,0:T(4,128)S(1)}, f32[8,3,256]{2,1,0:T(4,128)S(1)}, f32[3,512]{1,0:T(4,128)S(1)}, /*index=5*/s32[]{:T(128)}) while((s32[]{:T(128)}, f32[8,3,256]{2,1,0:T(4,128)S(1)}, f32[3,512]{1,0:T(4,128)S(1)}, f32[8,3,256]{2,1,0:T(4,128)S(1)}, f32[3,512]{1,0:T(4,128)S(1)}, ...), condition=%wide.region_22.24_spmd, body=%wide.region_19.23_spmd.sunk | while | flops 4193538 | bytes 8433741 | solution.py:45
  145.7 4.1 %collective-permute-start.5 = (f32[6,512]{1,0:T(8,128)S(1)}, f32[6,512]{1,0:T(8,128)S(1)}, u32[]{:S(2)}, u32[]{:S(2)}) collective-permute-start(f32[6,512]{1,0:T(8,128)S(1)} %collective-permute-done.4), channel_id=1, source_target_pairs={{0,4},{4,8},{8,12},{12,16},{16,20},{20,24},{24,28},{28,32},{32,36}... | collective-permute-start | bytes 36872 | tf_op jit(solution)/shard_map/ppermute | solution.py:20
  149.8 8.1 %while.85 = (s32[]{:T(128)}, f32[8,3,256]{2,1,0:T(4,128)S(1)}, f32[3,512]{1,0:T(4,128)S(1)}, f32[8,3,256]{2,1,0:T(4,128)S(1)}, f32[3,512]{1,0:T(4,128)S(1)}, /*index=5*/s32[]{:T(128)}) while((s32[]{:T(128)}, f32[8,3,256]{2,1,0:T(4,128)S(1)}, f32[3,512]{1,0:T(4,128)S(1)}, f32[8,3,256]{2,1,0:T(4,128)S(1)}, f32[3,512]{1,0:T(4,128)S(1)}, ...), condition=%wide.region_26.28_spmd, body=%wide.region_23.27_spmd.sunk | while | flops 4193538 | bytes 8433741 | solution.py:45
  157.9 2.9 %collective-permute-start.6 = (f32[6,512]{1,0:T(8,128)S(1)}, f32[6,512]{1,0:T(8,128)S(1)}, u32[]{:S(2)}, u32[]{:S(2)}) collective-permute-start(f32[6,512]{1,0:T(8,128)S(1)} %collective-permute-done.5), channel_id=1, source_target_pairs={{0,4},{4,8},{8,12},{12,16},{16,20},{20,24},{24,28},{28,32},{32,36}... | collective-permute-start | bytes 36872 | tf_op jit(solution)/shard_map/ppermute | solution.py:20
  160.9 8.1 %while.86 = (s32[]{:T(128)}, f32[8,3,256]{2,1,0:T(4,128)S(1)}, f32[3,512]{1,0:T(4,128)S(1)}, f32[8,3,256]{2,1,0:T(4,128)S(1)}, f32[3,512]{1,0:T(4,128)S(1)}, /*index=5*/s32[]{:T(128)}) while((s32[]{:T(128)}, f32[8,3,256]{2,1,0:T(4,128)S(1)}, f32[3,512]{1,0:T(4,128)S(1)}, f32[8,3,256]{2,1,0:T(4,128)S(1)}, f32[3,512]{1,0:T(4,128)S(1)}, ...), condition=%wide.region_30.32_spmd, body=%wide.region_27.31_spmd.sunk | while | flops 4193538 | bytes 8433741 | solution.py:45
  169.0 8.1 %while.87 = (s32[]{:T(128)}, f32[8,3,256]{2,1,0:T(4,128)S(1)}, f32[3,512]{1,0:T(4,128)S(1)}, f32[8,3,256]{2,1,0:T(4,128)S(1)}, f32[3,512]{1,0:T(4,128)S(1)}, /*index=5*/s32[]{:T(128)}) while((s32[]{:T(128)}, f32[8,3,256]{2,1,0:T(4,128)S(1)}, f32[3,512]{1,0:T(4,128)S(1)}, f32[8,3,256]{2,1,0:T(4,128)S(1)}, f32[3,512]{1,0:T(4,128)S(1)}, ...), condition=%wide.region_34.36_spmd, body=%wide.region_31.35_spmd.sunk | while | flops 4193538 | bytes 8433741 | solution.py:45
  177.1 23.2 %psum.7 = f32[3,2048]{1,0:T(4,128)S(1)} all-reduce(f32[3,2048]{1,0:T(4,128)S(1)} %bitcast.204), channel_id=1, replica_groups=mesh['blk'=128,'rep'=4] {'rep'}, use_global_device_ids=true, to_apply=%region_35.37 | all-reduce | flops 6144 | bytes 49152 | tf_op jit(solution)/shard_map/psum | solution.py:107
  (522 shorter events, 67.3 us)
Async XLA Ops:
  0.0 24.0 %copy-start = (f32[3,512]{1,0:T(4,128)S(1)}, f32[3,512]{1,0:T(4,128)}, u32[]{:S(2)}) copy-start(f32[3,512]{1,0:T(4,128)} %param.25) | copy-start | bytes 18436
  0.0 23.4 %copy-start.1 = (s32[1280]{0:T(1024)S(1)}, s32[1280]{0:T(1024)}, u32[]{:S(2)}) copy-start(s32[1280]{0:T(1024)} %param.29) | copy-start | bytes 15364
  0.0 23.4 %copy-start.3 = (s32[1280]{0:T(1024)S(1)}, s32[1280]{0:T(1024)}, u32[]{:S(2)}) copy-start(s32[1280]{0:T(1024)} %param.30) | copy-start | bytes 15364
  0.0 23.4 %copy-start.2 = (s32[1280]{0:T(1024)S(1)}, s32[1280]{0:T(1024)}, u32[]{:S(2)}) copy-start(s32[1280]{0:T(1024)} %param.31) | copy-start | bytes 15364
  4.8 31.6 %all-to-all-start = ((f32[3,128,10]{2,0,1:T(4,128)}), f32[3,128,10]{2,0,1:T(4,128)S(1)}, u32[]{:S(2)}, u32[]{:S(2)}) async-start(f32[3,128,10]{2,0,1:T(4,128)} %copy.149), calls=%async_computation | async-start | bytes 524288 | tf_op jit(solution)/shard_map/all_to_all | solution.py:71
  58.1 29.6 %all-to-all-start.1 = ((f32[6,128,10]{2,0,1:T(8,128)}), f32[6,128,10]{2,0,1:T(8,128)S(1)}, u32[]{:S(2)}, u32[]{:S(2)}) async-start(f32[6,128,10]{2,0,1:T(8,128)} %copy.163), calls=%async_computation.1 | async-start | bytes 1048576 | tf_op jit(solution)/shard_map/all_to_all | solution.py:84
  89.6 13.6 %collective-permute-start = (f32[6,512]{1,0:T(8,128)S(1)}, f32[6,512]{1,0:T(8,128)S(1)}, u32[]{:S(2)}, u32[]{:S(2)}) collective-permute-start(f32[6,512]{1,0:T(8,128)S(1)} %pad_maximum_fusion.1), channel_id=1, source_target_pairs={{0,508},{4,0},{8,4},{12,8},{16,12},{20,16},{24,20},{28,24},{32,28}... | collective-permute-start | bytes 36872 | tf_op jit(solution)/shard_map/ppermute | solution.py:20
  103.2 10.5 %collective-permute-start.1 = (f32[6,512]{1,0:T(8,128)S(1)}, f32[6,512]{1,0:T(8,128)S(1)}, u32[]{:S(2)}, u32[]{:S(2)}) collective-permute-start(f32[6,512]{1,0:T(8,128)S(1)} %collective-permute-done), channel_id=1, source_target_pairs={{0,508},{4,0},{8,4},{12,8},{16,12},{20,16},{24,20},{28,24},{32,28}... | collective-permute-start | bytes 36872 | tf_op jit(solution)/shard_map/ppermute | solution.py:20
  113.6 10.5 %collective-permute-start.2 = (f32[6,512]{1,0:T(8,128)S(1)}, f32[6,512]{1,0:T(8,128)S(1)}, u32[]{:S(2)}, u32[]{:S(2)}) collective-permute-start(f32[6,512]{1,0:T(8,128)S(1)} %collective-permute-done.1), channel_id=1, source_target_pairs={{0,508},{4,0},{8,4},{12,8},{16,12},{20,16},{24,20},{28,24},{32,28}... | collective-permute-start | bytes 36872 | tf_op jit(solution)/shard_map/ppermute | solution.py:20
  124.1 10.5 %collective-permute-start.3 = (f32[6,512]{1,0:T(8,128)S(1)}, f32[6,512]{1,0:T(8,128)S(1)}, u32[]{:S(2)}, u32[]{:S(2)}) collective-permute-start(f32[6,512]{1,0:T(8,128)S(1)} %collective-permute-done.2), channel_id=1, source_target_pairs={{0,508},{4,0},{8,4},{12,8},{16,12},{20,16},{24,20},{28,24},{32,28}... | collective-permute-start | bytes 36872 | tf_op jit(solution)/shard_map/ppermute | solution.py:20
  134.6 11.1 %collective-permute-start.4 = (f32[6,512]{1,0:T(8,128)S(1)}, f32[6,512]{1,0:T(8,128)S(1)}, u32[]{:S(2)}, u32[]{:S(2)}) collective-permute-start(f32[6,512]{1,0:T(8,128)S(1)} %collective-permute-done.3), channel_id=1, source_target_pairs={{0,20},{4,24},{8,28},{12,32},{16,36},{20,40},{24,44},{28,48},{32,5... | collective-permute-start | bytes 36872 | tf_op jit(solution)/shard_map/ppermute | solution.py:20
  145.7 12.2 %collective-permute-start.5 = (f32[6,512]{1,0:T(8,128)S(1)}, f32[6,512]{1,0:T(8,128)S(1)}, u32[]{:S(2)}, u32[]{:S(2)}) collective-permute-start(f32[6,512]{1,0:T(8,128)S(1)} %collective-permute-done.4), channel_id=1, source_target_pairs={{0,4},{4,8},{8,12},{12,16},{16,20},{20,24},{24,28},{28,32},{32,36}... | collective-permute-start | bytes 36872 | tf_op jit(solution)/shard_map/ppermute | solution.py:20
  157.9 11.0 %collective-permute-start.6 = (f32[6,512]{1,0:T(8,128)S(1)}, f32[6,512]{1,0:T(8,128)S(1)}, u32[]{:S(2)}, u32[]{:S(2)}) collective-permute-start(f32[6,512]{1,0:T(8,128)S(1)} %collective-permute-done.5), channel_id=1, source_target_pairs={{0,4},{4,8},{8,12},{12,16},{16,20},{20,24},{24,28},{28,32},{32,36}... | collective-permute-start | bytes 36872 | tf_op jit(solution)/shard_map/ppermute | solution.py:20
  169.0 31.3 %copy-start.4 = (f32[3,512]{1,0:T(4,128)S(1)}, f32[3,512]{1,0:T(4,128)}, u32[]{:S(2)}) copy-start(f32[3,512]{1,0:T(4,128)} %param.26) | copy-start | bytes 18436
where the time goes:
time: 202 us; the launch traced here: 201 us
  other arithmetic  61.1 us (30%)
  starting transfers between devices  52 us (26%)
  blocking collectives  33 us (16%)
  local copies, waits for them, and re-layouts  29.2 us (14%)
  waiting for transfers between devices  21.3 us (11%)
  loops' own time  3.7 us (2%)
    psum x1, blocking collectives, shards(): summed_group = lax.psum(far_total, 'rep')  23.2 us
    ppermute x7, starting transfers between devices, passed_along(): return lax.ppermute(value, axis, pairs)  21.9 us
    all_to_all x1, starting transfers between devices, shards(): lax.all_to_all(outgoing.reshape(3, owners, capacity), 'blk', split_axis=1...  18.6 us
    all_to_all x1, waiting for transfers between devices, shards(): lax.all_to_all(leaving.reshape(6, owners, capacity), 'blk', split_axis=1,...  18.1 us
    sub x66, other arithmetic, cross_product(): left[1] * right[2] - left[2] * right[1]  17 us
    reduce_sum x64, other arithmetic, one_block(): radius_sq = jnp.sum(separation * separation, axis=0) + CORE_SQUARED  15.1 us
    reduce_sum x64, other arithmetic, one_block(): return jnp.sum(turned * weight[None], axis=2)  14.8 us
    div x64, other arithmetic, one_block(): weight = 1.0 / (radius_sq * jnp.sqrt(radius_sq))  12.3 us
  transfers between devices with their start and end apart: 9, of which 3 were waited for; matrix products, arithmetic and copies ran while one was open for 27% of the time, Pallas kernels for 0%

commit v1 on v0

v1 whole, which is shorter than its diff:
```python
import functools

import jax
import jax.numpy as jnp
from jax import lax
from jax.experimental import pallas as pl
from jax.experimental.pallas import tpu as pltpu
from jax.sharding import PartitionSpec as P

LOCAL_BETA = 0.3
FRICTION_ALPHA = 0.21
FRICTION_PRIME = 0.06
BIOT_SCALE = 0.01
CORE_SQUARED = 0.25
SPEED_FLOOR = 1.0

BLOCKS = 128
LINE = 8
PLANES = BLOCKS // LINE
REPS = 4
STOPS = 8
BACK = STOPS // 2 - 1
SOURCES = STOPS * REPS
PT = 512
CAP = 10
LANES = 128
SLOT_ROWS = 8
COLUMN_ROWS = 10

MESH = pl.DeviceIdType.MESH
F32 = jnp.float32
BF16 = jnp.bfloat16
I32 = jnp.int32

NT = (((1,), (1,)), ((), ()))
NN = (((1,), (0,)), ((), ()))


def dot(left, right, dims=NN):
    return lax.dot_general(left, right, dims, preferred_element_type=F32)


def rounded(value):
    return value.astype(BF16).astype(F32)


def split(value):
    high = rounded(value)
    rest = value - high
    mid = rounded(rest)
    return high, mid, rest - mid


def iota(shape, dim):
    return lax.broadcasted_iota(I32, shape, dim)


def pick(table, index):
    return jnp.take_along_axis(table, index, axis=1, mode="promise_in_bounds")


def look_up(table, index):
    row, lane = index >> 7, index & 127
    found = jnp.zeros(index.shape, table.dtype)
    for t in range(COLUMN_ROWS):
        piece = jnp.broadcast_to(table[t : t + 1], index.shape)
        found = jnp.where(row == t, pick(piece, lane), found)
    return found


def stop_of(step):
    odd = step % 2
    return odd * ((step + 1) // 2) - (1 - odd) * (step // 2)


def kernel(
    pos_ref, flow_ref, owner_ref, slot_ref, recv_ref, order_ref, count_ref, out_ref,
    out1, in1, turned1, arrived, out2, in2, turned2, returned,
    src_pos, src_tan, target, w_high, w_low, total, index_a, index_b, member,
    send_sem, sem1, sem2, sem3, sem4, pos_sem, tan_sem,
):
    me = lax.axis_index("blk")
    rep = lax.axis_index("rep")
    plane = me // LINE
    place = me % LINE
    mine = BACK * REPS + rep

    def on_line(k):
        return (place + k) % LINE

    def on_plane(k):
        return (plane + k) % PLANES

    def source(step):
        stop = stop_of(step // REPS)
        other = (rep + step % REPS) % REPS
        return stop, other

    barrier = pltpu.get_barrier_semaphore()

    def greet(blk, other):
        pl.semaphore_signal(barrier, inc=1, device_id=(blk, other), device_id_type=MESH)

    for k in range(1, LINE):
        greet(plane * LINE + on_line(k), rep)
    for k in range(1, PLANES):
        greet(on_plane(k) * LINE + place, rep)

    def greet_source(step, carry):
        stop, other = source(step)
        greet((me + stop + BLOCKS) % BLOCKS, other)
        return carry

    lax.fori_loop(1, SOURCES, greet_source, 0)

    pos = pos_ref[...]
    square = jnp.sum(pos * pos, axis=0, keepdims=True)
    src_pos[mine] = jnp.concatenate([pos, square], axis=0)

    owner = owner_ref[...]
    slot = slot_ref[...]
    owner_row = (owner & (LINE - 1)) * PLANES + (owner >> 3)
    is_owner = jnp.where(iota((BLOCKS, PT), 0) == owner_row, 1.0, 0.0).astype(BF16)
    member[...] = is_owner
    pos_twice = jnp.concatenate([pos, pos, jnp.zeros((2, PT), F32)], axis=0)
    slotted = jnp.concatenate(
        [jnp.where(slot == s, pos_twice, 0.0) for s in range(CAP)]
        + [jnp.zeros((LANES - CAP * SLOT_ROWS, PT), F32)],
        axis=0,
    )
    outgoing = sum(dot(is_owner, part.astype(BF16), NT) for part in split(slotted))
    out1[...] = outgoing.reshape(LINE, PLANES, LANES)

    ones = jnp.ones((1, PT), F32)
    none = jnp.zeros((3, PT), F32)
    wanted = jnp.concatenate([-2.0 * pos, ones, square + CORE_SQUARED, none], axis=0)
    th, tm, tl = split(wanted)
    features = jnp.concatenate(
        [th, th, tm, tm, th, tl, tl, tm, jnp.zeros((LANES - 64, PT), F32)], axis=0
    )
    target[...] = features.T.astype(BF16)
    one_row = jnp.concatenate([ones, none], axis=0)
    no_rows = jnp.zeros((LANES - 64, PT), F32)

    def weigh(n):
        sh, sm, sl = split(jnp.concatenate([src_pos[n], one_row], axis=0))
        rows = jnp.concatenate([sh, sm, sh, sm, sl, sh, sm, sl, no_rows], axis=0).astype(BF16)
        for half in range(PT // 256):
            columns = slice(half * 256, half * 256 + 256)
            root = lax.rsqrt(dot(target[...], rows[:, columns]))
            weight = root * root * root
            high = weight.astype(BF16)
            w_high[n, :, columns] = high
            w_low[n, :, columns] = (weight - high.astype(F32)).astype(BF16)

    def block_copy(ref, sem, send, step):
        stop, other = source(step)
        return pltpu.make_async_remote_copy(
            src_ref=ref.at[mine],
            dst_ref=ref.at[(stop + BACK) * REPS + rep],
            send_sem=send,
            recv_sem=sem.at[(stop + BACK) * REPS + rep],
            device_id=((me - stop + BLOCKS) % BLOCKS, other),
            device_id_type=MESH,
        )

    def arriving(ref, sem, send, step):
        stop, other = source(step)
        n = (stop + BACK) * REPS + other
        pltpu.make_async_remote_copy(
            src_ref=ref.at[n],
            dst_ref=ref.at[n],
            send_sem=send,
            recv_sem=sem.at[n],
            device_id=(me, rep),
            device_id_type=MESH,
        ).wait_recv()
        return n

    def send_blocks(ref, sem, send, low, top):
        def one(step, carry):
            block_copy(ref, sem, send, step).start()
            return carry

        lax.fori_loop(low, top, one, 0)

    def weigh_steps(low, top):
        def one(step, carry):
            weigh(arriving(src_pos, pos_sem, send_sem.at[4], step))
            return carry

        lax.fori_loop(low, top, one, 0)

    def line_copy(src, dst, sem, send, k):
        there = on_line(k)
        return pltpu.make_async_remote_copy(
            src_ref=src.at[there],
            dst_ref=dst.at[place],
            send_sem=send,
            recv_sem=sem.at[place],
            device_id=(plane * LINE + there, rep),
            device_id_type=MESH,
        )

    def plane_copy(src, dst, sem, send, k):
        there = on_plane(k)
        return pltpu.make_async_remote_copy(
            src_ref=src.at[there],
            dst_ref=dst.at[plane],
            send_sem=send,
            recv_sem=sem.at[plane],
            device_id=(there * LINE + place, rep),
            device_id_type=MESH,
        )

    def await_piece(dst, sem, send, n):
        pltpu.make_async_remote_copy(
            src_ref=dst.at[n],
            dst_ref=dst.at[n],
            send_sem=send,
            recv_sem=sem.at[n],
            device_id=(me, rep),
            device_id_type=MESH,
        ).wait_recv()

    def await_sent(ref, count, send):
        pltpu.make_async_remote_copy(
            src_ref=ref.at[pl.ds(0, count)],
            dst_ref=ref.at[pl.ds(0, count)],
            send_sem=send,
            recv_sem=sem1.at[0],
            device_id=(me, rep),
            device_id_type=MESH,
        ).wait_send()

    pl.semaphore_wait(barrier, (LINE - 1) + (PLANES - 1) + (SOURCES - 1))

    for k in range(1, LINE):
        line_copy(out1, in1, sem1, send_sem.at[0], k).start()
    in1[place] = out1[place]
    send_blocks(src_pos, pos_sem, send_sem.at[4], 1, 8)

    spot = iota((16, LANES), 1) * CAP + iota((16, LANES), 0)
    column = jnp.where(iota((16, LANES), 0) < CAP, look_up(recv_ref[...], spot), -1)
    column_row, column_lane = column >> 7, column & 127
    holder = iota((16, LANES), 1).astype(F32)
    inverse = jnp.zeros((32, LANES), F32)
    for s in range(CAP):
        hit = column_row[s : s + 1] == iota((16, LANES), 0)
        left = jnp.concatenate(
            [jnp.where(hit, holder, 0.0), jnp.where(hit, float(s), 0.0)], axis=0
        ).astype(BF16)
        right = jnp.where(column_lane[s : s + 1] == iota((LANES, LANES), 0), 1.0, 0.0).astype(BF16)
        inverse = inverse + dot(left, right, NT)
    inverse = (inverse[16:] * float(LANES) + inverse[:16]).astype(I32)
    at = jnp.maximum(column, 0)
    order = look_up(order_ref[...], at)
    count = look_up(count_ref[...], at)

    def neighbour(offset):
        moved = order + offset
        moved = jnp.where(moved < 0, moved + count, jnp.where(moved >= count, moved - count, moved))
        there = jnp.clip(at - order + moved, 0, COLUMN_ROWS * LANES - 1)
        return look_up(inverse, there)

    ahead1, ahead2, behind1, behind2 = (neighbour(k) for k in (1, 2, -1, -2))
    near = iota((SLOT_ROWS, LANES), 0) < 3
    for s in range(CAP):
        index_a[s] = jnp.where(near, ahead1[s : s + 1], ahead2[s : s + 1])
        index_b[s] = jnp.where(near, behind1[s : s + 1], behind2[s : s + 1])

    for k in range(1, LINE):
        await_piece(in1, sem1, send_sem.at[0], on_line(k))
    for j in range(PLANES):
        turned1[j] = in1[:, j, :]
    for k in range(1, PLANES):
        plane_copy(turned1, arrived, sem2, send_sem.at[1], k).start()
    arrived[plane] = turned1[plane]
    send_blocks(src_pos, pos_sem, send_sem.at[4], 8, 20)
    weigh(mine)
    weigh_steps(1, 4)

    for k in range(1, PLANES):
        await_piece(arrived, sem2, send_sem.at[1], on_plane(k))
    tables = arrived[...].reshape(BLOCKS, LANES).T
    middle = iota((SLOT_ROWS, LANES), 0) < 6
    results = []
    for s in range(CAP):
        to_a, to_b = index_a[s], index_b[s]
        row_a, row_b, lane_a, lane_b = to_a >> 7, to_b >> 7, to_a & 127, to_b & 127
        after = jnp.zeros((SLOT_ROWS, LANES), F32)
        before = jnp.zeros((SLOT_ROWS, LANES), F32)
        for t in range(CAP):
            table = tables[t * SLOT_ROWS : (t + 1) * SLOT_ROWS]
            after = jnp.where(row_a == t, pick(table, lane_a), after)
            before = jnp.where(row_b == t, pick(table, lane_b), before)
        here = tables[s * SLOT_ROWS : (s + 1) * SLOT_ROWS]
        gap, both = after - before, after + before
        first = 8.0 * gap - pltpu.roll(gap, SLOT_ROWS - 3, 0)
        second = 16.0 * pltpu.roll(both, 3, 0) - both - 30.0 * here
        results.append(jnp.where(near, first, jnp.where(middle, second, 0.0)) / 12.0)
    results.append(jnp.zeros((LANES - CAP * SLOT_ROWS, LANES), F32))
    out2[...] = jnp.concatenate(results, axis=0).T.reshape(PLANES, LINE, LANES)

    for k in range(1, PLANES):
        plane_copy(out2, in2, sem3, send_sem.at[2], k).start()
    in2[plane] = out2[plane]
    send_blocks(src_pos, pos_sem, send_sem.at[4], 20, SOURCES)
    weigh_steps(4, 8)

    for k in range(1, PLANES):
        await_piece(in2, sem3, send_sem.at[2], on_plane(k))
    for j in range(LINE):
        turned2[j] = in2[:, j, :]
    for k in range(1, LINE):
        line_copy(turned2, returned, sem4, send_sem.at[3], k).start()
    returned[place] = turned2[place]
    weigh_steps(8, 12)

    for k in range(1, LINE):
        await_piece(returned, sem4, send_sem.at[3], on_line(k))
    back = returned[...].reshape(BLOCKS, LANES).T
    is_owner = member[...]
    spread = sum(dot(part.astype(BF16), is_owner) for part in split(back))
    derived = jnp.zeros((SLOT_ROWS, PT), F32)
    for s in range(CAP):
        derived = jnp.where(slot == s, spread[s * SLOT_ROWS : (s + 1) * SLOT_ROWS], derived)
    src_tan[mine] = jnp.concatenate([derived[0:3], jnp.zeros((1, PT), F32)], axis=0)
    send_blocks(src_tan, tan_sem, send_sem.at[5], 1, SOURCES)
    weigh_steps(12, SOURCES)

    def gather_sums(n):
        p, t = src_pos[n], src_tan[n]
        p0, p1, p2 = p[0:1], p[1:2], p[2:3]
        t0, t1, t2 = t[0:1], t[1:2], t[2:3]
        rows = jnp.concatenate(
            [t0, t1, t2, t1 * p2 - t2 * p1, t2 * p0 - t0 * p2, t0 * p1 - t1 * p0,
             jnp.zeros((2, PT), F32)],
            axis=0,
        )
        h, m, l = split(rows)
        right = jnp.concatenate([h, m, l, jnp.zeros((8, PT), F32)], axis=0).astype(BF16)
        return dot(w_high[n], right, NT) + dot(w_low[n], right, NT)

    total[...] = gather_sums(mine)

    def sum_step(step, carry):
        n = arriving(src_tan, tan_sem, send_sem.at[5], step)
        total[...] += gather_sums(n)
        return carry

    lax.fori_loop(1, SOURCES, sum_step, 0)
    sums = total[...].T
    sums = sums[0:8] + sums[8:16] + sums[16:24]

    def cross(a, b):
        return [
            a[1] * b[2] - a[2] * b[1],
            a[2] * b[0] - a[0] * b[2],
            a[0] * b[1] - a[1] * b[0],
        ]

    x = [pos[c : c + 1] for c in range(3)]
    flow = [flow_ref[c : c + 1, :] for c in range(3)]
    tangent = [derived[c : c + 1] for c in range(3)]
    curvature = [derived[c : c + 1] for c in range(3, 6)]
    far = cross([sums[c : c + 1] for c in range(3)], x)
    speed = jnp.maximum(
        tangent[0] * tangent[0] + tangent[1] * tangent[1] + tangent[2] * tangent[2], SPEED_FLOOR
    )
    per_speed = 1.0 / jnp.sqrt(speed)
    scale = LOCAL_BETA * per_speed / speed
    local = cross(tangent, curvature)
    superfluid = [
        scale * local[c] + BIOT_SCALE * (far[c] - sums[3 + c : 4 + c]) for c in range(3)
    ]
    unit = [tangent[c] * per_speed for c in range(3)]
    once = cross(unit, [flow[c] - superfluid[c] for c in range(3)])
    twice = cross(unit, once)
    for c in range(3):
        out_ref[c : c + 1, :] = (
            superfluid[c] + FRICTION_ALPHA * once[c] - FRICTION_PRIME * twice[c]
        )

    await_sent(out1, LINE - 1, send_sem.at[0])
    await_sent(turned1, PLANES - 1, send_sem.at[1])
    await_sent(out2, PLANES - 1, send_sem.at[2])
    await_sent(turned2, LINE - 1, send_sem.at[3])
    await_sent(src_pos, SOURCES - 1, send_sem.at[4])
    await_sent(src_tan, SOURCES - 1, send_sem.at[5])


def shards(positions, normal_flow, send_owner, send_slot, recv_index, loop_pos, loop_len):
    vmem = pl.BlockSpec(memory_space=pltpu.VMEM)
    dma = pltpu.SemaphoreType.DMA
    return pl.pallas_call(
        kernel,
        out_shape=jax.ShapeDtypeStruct((3, PT), F32),
        in_specs=[vmem] * 7,
        out_specs=vmem,
        scratch_shapes=[
            pltpu.VMEM((LINE, PLANES, LANES), F32),
            pltpu.VMEM((LINE, PLANES, LANES), F32),
            pltpu.VMEM((PLANES, LINE, LANES), F32),
            pltpu.VMEM((PLANES, LINE, LANES), F32),
            pltpu.VMEM((PLANES, LINE, LANES), F32),
            pltpu.VMEM((PLANES, LINE, LANES), F32),
            pltpu.VMEM((LINE, PLANES, LANES), F32),
            pltpu.VMEM((LINE, PLANES, LANES), F32),
            pltpu.VMEM((SOURCES, 4, PT), F32),
            pltpu.VMEM((SOURCES, 4, PT), F32),
            pltpu.VMEM((PT, LANES), BF16),
            pltpu.VMEM((SOURCES, PT, PT), BF16),
            pltpu.VMEM((SOURCES, PT, PT), BF16),
            pltpu.VMEM((PT, 32), F32),
            pltpu.VMEM((CAP, SLOT_ROWS, LANES), I32),
            pltpu.VMEM((CAP, SLOT_ROWS, LANES), I32),
            pltpu.VMEM((BLOCKS, PT), BF16),
            dma((6,)),
            dma((LINE,)),
            dma((PLANES,)),
            dma((PLANES,)),
            dma((LINE,)),
            dma((SOURCES,)),
            dma((SOURCES,)),
        ],
        compiler_params=pltpu.CompilerParams(
            collective_id=0, has_side_effects=True, vmem_limit_bytes=56 * 1024 * 1024
        ),
        cost_estimate=pl.CostEstimate(
            flops=2 * PT * SOURCES * PT * 128, bytes_accessed=1 << 20, transcendentals=PT * SOURCES * PT
        ),
    )(
        positions,
        normal_flow,
        send_owner.reshape(1, PT),
        send_slot.reshape(1, PT),
        recv_index.reshape(CAP, BLOCKS),
        loop_pos.reshape(COLUMN_ROWS, LANES),
        loop_len.reshape(COLUMN_ROWS, LANES),
    )


def solution(mesh):
    both = P(("blk", "rep"))
    wide = P(None, ("blk", "rep"))
    return jax.shard_map(
        shards,
        mesh=mesh,
        in_specs=(wide, wide, both, both, both, both, both),
        out_specs=wide,
        check_vma=False,
    )
```

time: 202 us -> 66.5 us (0.33)
  Pallas kernels: 0 us -> 64.6 us
  other arithmetic: 61.1 us -> 0 us
  starting transfers between devices: 52 us -> 0 us
  blocking collectives: 33 us -> 0 us
  local copies, waits for them, and re-layouts: 29.2 us -> 1.3 us
  waiting for transfers between devices: 21.3 us -> 0 us
  loops' own time: 3.7 us -> 0 us
    pallas_call x0 -> x1, Pallas kernels: none -> 64.6 us  [shards(): pl.pallas_call(kernel, out_shape=jax.ShapeDtypeStruct((3, PT), F32), in_s...]
    all_to_all x2 -> x0, starting transfers between devices: 30.1 us -> none  [the longest x1 18.6 us: shards(): lax.all_to_all(outgoing.reshape(3, owners, capacity), 'blk', split_axis=1...]
    reduce_sum x129 -> x0, other arithmetic: 29.9 us -> none  [the longest x64 15.1 us: one_block(): radius_sq = jnp.sum(separation * separation, axis=0) + CORE_SQUARED]
    psum x1 -> x0, blocking collectives: 23.2 us -> none  [shards(): summed_group = lax.psum(far_total, 'rep')]
    ppermute x7 -> x0, starting transfers between devices: 21.9 us -> none  [passed_along(): return lax.ppermute(value, axis, pairs)]
    all_to_all x2 -> x0, waiting for transfers between devices: 20.6 us -> none  [the longest x1 18.1 us: shards(): lax.all_to_all(leaving.reshape(6, owners, capacity), 'blk', split_axis=1,...]
    sub x70 -> x0, other arithmetic: 17.6 us -> none  [the longest x66 17 us: cross_product(): left[1] * right[2] - left[2] * right[1]]
    gather x13 -> x0, local copies, waits for them, and re-layouts: 14.4 us -> none  [the longest x8 10.3 us: neighbour(): jnp.take(owned, loop_start + jnp.remainder(loop_pos + offset, loop_len),...]
  transfers between devices with their start and end apart: 9 -> 0, of which waited for: 3 -> 0; matrix products, arithmetic and copies ran while one was open for 27% -> 0% of each run, Pallas kernels for 0% -> 0%
where the time goes in v1:
time: 66.5 us; the launch traced here: 65.9 us
  Pallas kernels  64.6 us (97%)
  local copies, waits for them, and re-layouts  1.3 us (2%)
    pallas_call x1, Pallas kernels, shards(): pl.pallas_call(kernel, out_shape=jax.ShapeDtypeStruct((3, PT), F32), in_s...  64.6 us

profile of v1, /device:TPU:1, one launch (start us, length us, event | category | flops | bytes accessed | tf_op | source)
XLA Modules:
  0.0 65.9 jit_solution(15975507654303842784)
XLA Ops:
  0.0 64.6 %shard_map.73 = f32[3,512]{1,0:T(4,128)} custom-call(f32[3,512]{1,0:T(4,128)} %pos_ref.1, f32[3,512]{1,0:T(4,128)} %flow_ref.1, s32[1,512]{1,0:T(1,128)} %bitcast.8, s32[1,512]{1,0:T(1,128)} %bitcast.9, s32[10,128]{1,0:T(8,128)} %bitcast.5, s32[10,128]{1,0:T(8,128)} %bitcast.6, s32[10,128]{1,0:T(8,128)} %bitcast.7), custom_call_target="tpu_custom_call" | custom-call | flops 2147483648 | bytes 1048576 | tf_op jit(solution)/shard_map/pallas_call | solution.py:396
  64.6 1.3 %copy.9 = f32[3,512]{1,0:T(4,128)} copy(f32[3,512]{1,0:T(4,128)} %shard_map.73) | data formatting | bytes 12288

commit v2 on v1

v2 whole, which is shorter than its diff:
```python
import functools

import jax
import jax.numpy as jnp
from jax import lax
from jax.experimental import pallas as pl
from jax.experimental.pallas import tpu as pltpu
from jax.sharding import PartitionSpec as P

LOCAL_BETA = 0.3
FRICTION_ALPHA = 0.21
FRICTION_PRIME = 0.06
BIOT_SCALE = 0.01
CORE_SQUARED = 0.25
SPEED_FLOOR = 1.0

BLOCKS = 128
LINE = 8
PLANES = BLOCKS // LINE
REPS = 4
STOPS = 8
BACK = STOPS // 2 - 1
SOURCES = STOPS * REPS
PT = 512
CAP = 10
LANES = 128
SLOT_ROWS = 8
COLUMN_ROWS = 10

FEATURES = 64
STOP_ORDER = (0, 1, -1, 2, -2, 3, -3, 4)

MESH = pl.DeviceIdType.MESH
F32 = jnp.float32
BF16 = jnp.bfloat16
I32 = jnp.int32

NT = (((1,), (1,)), ((), ()))
NN = (((1,), (0,)), ((), ()))


def dot(left, right, dims=NN):
    return lax.dot_general(left, right, dims, preferred_element_type=F32)


def rounded(value):
    return value.astype(BF16).astype(F32)


def split(value):
    high = rounded(value)
    rest = value - high
    mid = rounded(rest)
    return high, mid, rest - mid


def iota(shape, dim):
    return lax.broadcasted_iota(I32, shape, dim)


def pick(table, index):
    return jnp.take_along_axis(table, index, axis=1, mode="promise_in_bounds")


def look_up(table, index):
    row, lane = index >> 7, index & 127
    found = jnp.zeros(index.shape, table.dtype)
    for t in range(COLUMN_ROWS):
        piece = jnp.broadcast_to(table[t : t + 1], index.shape)
        found = jnp.where(row == t, pick(piece, lane), found)
    return found


def cross(a, b):
    return [
        a[1] * b[2] - a[2] * b[1],
        a[2] * b[0] - a[0] * b[2],
        a[0] * b[1] - a[1] * b[0],
    ]


def rows_of(value, low, top):
    return [value[c : c + 1] for c in range(low, top)]


def kernel(
    pos_hbm, flow_hbm, owner_hbm, slot_hbm, recv_hbm, order_hbm, count_hbm, out_ref,
    pos_ref, flow_ref, owner_ref, slot_ref, recv_ref, order_ref, count_ref,
    out1, in1, turned1, arrived, out2, in2, turned2, returned,
    targets, src_pos, src_tan, target, weights, right, total, part_out, part_in,
    index_a, index_b, member,
    load_sem, send_sem, phase_sem, rep_sem, pos_sem, tan_sem, part_sem,
):
    me = lax.axis_index("blk")
    rep = lax.axis_index("rep")
    plane = me // LINE
    place = me % LINE

    def on_line(k):
        return (place + k) % LINE

    def on_plane(k):
        return (plane + k) % PLANES

    def on_rep(k):
        return (rep + k) % REPS

    def block(stop):
        return (me + stop + BLOCKS) % BLOCKS

    barrier = pltpu.get_barrier_semaphore()

    def greet(blk, other):
        pl.semaphore_signal(barrier, inc=1, device_id=(blk, other), device_id_type=MESH)

    for k in range(1, LINE):
        greet(plane * LINE + on_line(k), rep)
    for k in range(1, PLANES):
        greet(on_plane(k) * LINE + place, rep)
    for k in range(1, REPS):
        greet(me, on_rep(k))
    for stop in STOP_ORDER[1:]:
        greet(block(stop), rep)

    loads = [
        pltpu.make_async_copy(src, dst, load_sem.at[i])
        for i, (src, dst) in enumerate(
            [
                (pos_hbm, pos_ref), (owner_hbm, owner_ref), (slot_hbm, slot_ref),
                (recv_hbm, recv_ref), (order_hbm, order_ref), (count_hbm, count_ref),
                (flow_hbm, flow_ref),
            ]
        )
    ]
    for load in loads:
        load.start()
    for load in loads[:3]:
        load.wait()

    pos = pos_ref[...]
    owner = owner_ref[...]
    slot = slot_ref[...]
    owner_row = (owner & (LINE - 1)) * PLANES + (owner >> 3)
    is_owner = jnp.where(iota((BLOCKS, PT), 0) == owner_row, 1.0, 0.0).astype(BF16)
    member[...] = is_owner
    pos_twice = jnp.concatenate([pos, pos, jnp.zeros((2, PT), F32)], axis=0)
    slotted = jnp.concatenate(
        [jnp.where(slot == s, pos_twice, 0.0) for s in range(CAP)]
        + [jnp.zeros((LANES - CAP * SLOT_ROWS, PT), F32)],
        axis=0,
    )
    outgoing = sum(dot(is_owner, part.astype(BF16), NT) for part in split(slotted))
    out1[...] = outgoing.reshape(LINE, PLANES, LANES)
    square = jnp.sum(pos * pos, axis=0, keepdims=True)
    pos_rows = jnp.concatenate([pos, square], axis=0)
    src_pos[BACK] = pos_rows
    targets[rep] = pos_rows

    def copy_to(src, dst, send, recv, blk, other):
        pltpu.make_async_remote_copy(
            src_ref=src, dst_ref=dst, send_sem=send_sem.at[send], recv_sem=recv,
            device_id=(blk, other), device_id_type=MESH,
        ).start()

    def send_line(src, dst, phase):
        for k in range(1, LINE):
            there = on_line(k)
            copy_to(src.at[there], dst.at[place], phase, phase_sem.at[phase],
                    plane * LINE + there, rep)

    def send_plane(src, dst, phase):
        for k in range(1, PLANES):
            there = on_plane(k)
            copy_to(src.at[there], dst.at[plane], phase, phase_sem.at[phase],
                    there * LINE + place, rep)

    def await_here(dst, recv):
        pltpu.make_async_remote_copy(
            src_ref=dst, dst_ref=dst, send_sem=send_sem.at[0], recv_sem=recv,
            device_id=(me, rep), device_id_type=MESH,
        ).wait_recv()

    def await_sent(part, send):
        pltpu.make_async_remote_copy(
            src_ref=part, dst_ref=part, send_sem=send_sem.at[send], recv_sem=phase_sem.at[0],
            device_id=(me, rep), device_id_type=MESH,
        ).wait_send()

    ones = jnp.ones((1, PT), F32)
    none = jnp.zeros((3, PT), F32)
    one_row = jnp.concatenate([ones, none], axis=0)

    def aim(other):
        rows = targets[other]
        wanted = jnp.concatenate(
            [-2.0 * rows[0:3], ones, rows[3:4] + CORE_SQUARED, none], axis=0
        )
        th, tm, tl = split(wanted)
        features = jnp.concatenate(
            [th, th, tm, tm, th, tl, tl, tm, jnp.zeros((LANES - FEATURES, PT), F32)], axis=0
        )
        target[other] = features.T[:, :FEATURES].astype(BF16)

    def weigh(stop, reps):
        sh, sm, sl = split(jnp.concatenate([src_pos[stop + BACK], one_row], axis=0))
        rows = jnp.concatenate([sh, sm, sh, sm, sl, sh, sm, sl], axis=0).astype(BF16)
        for k in reps:
            other = on_rep(k)
            for half in range(PT // 256):
                low, top = half * 256, half * 256 + 256
                root = lax.rsqrt(dot(target[other], rows[:, low:top]))
                weight = root * root * root
                high = weight.astype(BF16)
                weights[other, stop + BACK, :, low:top] = high
                weights[other, stop + BACK, :, PT + low : PT + top] = (
                    weight - high.astype(F32)
                ).astype(BF16)

    def weigh_stops(low, top):
        def one(i, carry):
            stop = (i % 2) * ((i + 1) // 2) - (1 - i % 2) * (i // 2)
            await_here(src_pos.at[stop + BACK], pos_sem.at[stop + BACK])
            weigh(stop, range(REPS))
            return carry

        lax.fori_loop(low, top, one, 0)

    aim(rep)
    weigh(0, [0])

    pl.semaphore_wait(barrier, (LINE - 1) + (PLANES - 1) + (REPS - 1) + (STOPS - 1))

    send_line(out1, in1, 0)
    for k in range(1, REPS):
        copy_to(targets.at[rep], targets.at[rep], 4, rep_sem.at[rep], me, on_rep(k))
    for stop in STOP_ORDER[1:]:
        copy_to(src_pos.at[BACK], src_pos.at[stop + BACK], 5, pos_sem.at[stop + BACK],
                block(-stop), rep)
    in1[place] = out1[place]

    for load in loads[3:]:
        load.wait()
    spot = iota((16, LANES), 1) * CAP + iota((16, LANES), 0)
    column = jnp.where(iota((16, LANES), 0) < CAP, look_up(recv_ref[...], spot), -1)
    column_row, column_lane = column >> 7, column & 127
    holder = iota((16, LANES), 1).astype(F32)
    inverse = jnp.zeros((32, LANES), F32)
    for s in range(CAP):
        hit = column_row[s : s + 1] == iota((16, LANES), 0)
        left = jnp.concatenate(
            [jnp.where(hit, holder, 0.0), jnp.where(hit, float(s), 0.0)], axis=0
        ).astype(BF16)
        lane_hit = column_lane[s : s + 1] == iota((LANES, LANES), 0)
        inverse = inverse + dot(left, jnp.where(lane_hit, 1.0, 0.0).astype(BF16), NT)
    inverse = (inverse[16:] * float(LANES) + inverse[:16]).astype(I32)
    at = jnp.maximum(column, 0)
    ring = look_up(order_ref[...] + (count_ref[...] << 11), at)
    order, count = ring & 2047, ring >> 11

    def neighbour(offset):
        moved = order + offset
        moved = jnp.where(moved < 0, moved + count, jnp.where(moved >= count, moved - count, moved))
        there = jnp.clip(at - order + moved, 0, COLUMN_ROWS * LANES - 1)
        return look_up(inverse, there)

    await_here(in1.at[pl.ds(0, LINE - 1)], phase_sem.at[0])
    for j in range(PLANES):
        turned1[j] = in1[:, j, :]
    send_plane(turned1, arrived, 1)
    arrived[plane] = turned1[plane]

    ahead1, ahead2, behind1, behind2 = (neighbour(k) for k in (1, 2, -1, -2))
    near = iota((SLOT_ROWS, LANES), 0) < 3
    for s in range(CAP):
        index_a[s] = jnp.where(near, ahead1[s : s + 1], ahead2[s : s + 1])
        index_b[s] = jnp.where(near, behind1[s : s + 1], behind2[s : s + 1])
    for k in range(1, REPS):
        await_here(targets.at[on_rep(k)], rep_sem.at[on_rep(k)])
        aim(on_rep(k))
    weigh(0, range(1, REPS))

    await_here(arrived.at[pl.ds(0, PLANES - 1)], phase_sem.at[1])
    tables = arrived[...].reshape(BLOCKS, LANES).T
    middle = iota((SLOT_ROWS, LANES), 0) < 6
    results = []
    for s in range(CAP):
        to_a, to_b = index_a[s], index_b[s]
        row_a, row_b, lane_a, lane_b = to_a >> 7, to_b >> 7, to_a & 127, to_b & 127
        after = jnp.zeros((SLOT_ROWS, LANES), F32)
        before = jnp.zeros((SLOT_ROWS, LANES), F32)
        for t in range(CAP):
            table = tables[t * SLOT_ROWS : (t + 1) * SLOT_ROWS]
            after = jnp.where(row_a == t, pick(table, lane_a), after)
            before = jnp.where(row_b == t, pick(table, lane_b), before)
        here = tables[s * SLOT_ROWS : (s + 1) * SLOT_ROWS]
        gap, both = after - before, after + before
        first = 8.0 * gap - pltpu.roll(gap, SLOT_ROWS - 3, 0)
        second = 16.0 * pltpu.roll(both, 3, 0) - both - 30.0 * here
        results.append(jnp.where(near, first, jnp.where(middle, second, 0.0)) / 12.0)
    results.append(jnp.zeros((LANES - CAP * SLOT_ROWS, LANES), F32))
    out2[...] = jnp.concatenate(results, axis=0).T.reshape(PLANES, LINE, LANES)

    send_plane(out2, in2, 2)
    in2[plane] = out2[plane]
    weigh_stops(1, 3)
    await_here(in2.at[pl.ds(0, PLANES - 1)], phase_sem.at[2])
    for j in range(LINE):
        turned2[j] = in2[:, j, :]
    send_line(turned2, returned, 3)
    returned[place] = turned2[place]
    weigh_stops(3, 5)
    await_here(returned.at[pl.ds(0, LINE - 1)], phase_sem.at[3])
    back = returned[...].reshape(BLOCKS, LANES).T
    is_owner = member[...]
    spread = sum(dot(part.astype(BF16), is_owner) for part in split(back))
    derived = jnp.zeros((SLOT_ROWS, PT), F32)
    for s in range(CAP):
        derived = jnp.where(slot == s, spread[s * SLOT_ROWS : (s + 1) * SLOT_ROWS], derived)

    src_tan[BACK] = jnp.concatenate([derived[0:3], jnp.zeros((1, PT), F32)], axis=0)
    for stop in STOP_ORDER[1:]:
        copy_to(src_tan.at[BACK], src_tan.at[stop + BACK], 6, tan_sem.at[stop + BACK],
                block(-stop), rep)
    weigh_stops(5, STOPS)

    def prepare(stop):
        p, t = rows_of(src_pos[stop], 0, 3), rows_of(src_tan[stop], 0, 3)
        h, m, l = split(jnp.concatenate(t + cross(t, p) + [jnp.zeros((2, PT), F32)], axis=0))
        rows = jnp.concatenate([h, m, l, jnp.zeros((8, PT), F32)], axis=0).astype(BF16)
        right[stop, :, :PT] = rows
        right[stop, :, PT:] = rows

    prepare(BACK)
    for stop in STOP_ORDER[1:]:
        await_here(src_tan.at[stop + BACK], tan_sem.at[stop + BACK])
        prepare(stop + BACK)

    def gather_sums(k):
        other = on_rep(k)
        total[...] = jnp.zeros_like(total)

        def one(i, carry):
            total[...] += dot(weights[other, 2 * i], right[2 * i], NT) + dot(
                weights[other, 2 * i + 1], right[2 * i + 1], NT
            )
            return carry

        lax.fori_loop(0, STOPS // 2, one, 0)
        parts = total[...].T
        parts = parts[0:8] + parts[8:16] + parts[16:24]
        far = cross(rows_of(parts, 0, 3), rows_of(targets[other], 0, 3))
        return [far[c] - parts[3 + c : 4 + c] for c in range(3)]

    for k in range(1, REPS):
        part_out[k - 1] = jnp.concatenate(gather_sums(k) + [jnp.zeros((1, PT), F32)], axis=0)
        copy_to(part_out.at[k - 1], part_in.at[k - 1], 7, part_sem.at[k - 1], me, on_rep(k))
    far = gather_sums(0)
    for k in range(1, REPS):
        await_here(part_in.at[k - 1], part_sem.at[k - 1])
    others = part_in[0] + part_in[1] + part_in[2]
    far = [far[c] + others[c : c + 1] for c in range(3)]

    tangent, curvature = rows_of(derived, 0, 3), rows_of(derived, 3, 6)
    speed = jnp.maximum(
        tangent[0] * tangent[0] + tangent[1] * tangent[1] + tangent[2] * tangent[2], SPEED_FLOOR
    )
    per_speed = 1.0 / jnp.sqrt(speed)
    scale = LOCAL_BETA * per_speed / speed
    local = cross(tangent, curvature)
    superfluid = [scale * local[c] + BIOT_SCALE * far[c] for c in range(3)]
    unit = [tangent[c] * per_speed for c in range(3)]
    once = cross(unit, [flow_ref[c : c + 1, :] - superfluid[c] for c in range(3)])
    twice = cross(unit, once)
    for c in range(3):
        out_ref[c : c + 1, :] = (
            superfluid[c] + FRICTION_ALPHA * once[c] - FRICTION_PRIME * twice[c]
        )

    await_sent(out1.at[pl.ds(0, LINE - 1)], 0)
    await_sent(turned1.at[pl.ds(0, PLANES - 1)], 1)
    await_sent(out2.at[pl.ds(0, PLANES - 1)], 2)
    await_sent(turned2.at[pl.ds(0, LINE - 1)], 3)
    await_sent(targets.at[pl.ds(0, REPS - 1)], 4)
    await_sent(src_pos.at[pl.ds(0, STOPS - 1)], 5)
    await_sent(src_tan.at[pl.ds(0, STOPS - 1)], 6)
    await_sent(part_out, 7)


def shards(positions, normal_flow, send_owner, send_slot, recv_index, loop_pos, loop_len):
    dma = pltpu.SemaphoreType.DMA
    by_line = pltpu.VMEM((LINE, PLANES, LANES), F32)
    by_plane = pltpu.VMEM((PLANES, LINE, LANES), F32)
    points = pltpu.VMEM((3, PT), F32)
    point_index = pltpu.VMEM((1, PT), I32)
    columns = pltpu.VMEM((COLUMN_ROWS, LANES), I32)
    return pl.pallas_call(
        kernel,
        out_shape=jax.ShapeDtypeStruct((3, PT), F32),
        in_specs=[pl.BlockSpec(memory_space=pltpu.HBM)] * 7,
        out_specs=pl.BlockSpec(memory_space=pltpu.VMEM),
        scratch_shapes=[
            points, points, point_index, point_index, columns, columns, columns,
            by_line, by_line, by_plane, by_plane, by_plane, by_plane, by_line, by_line,
            pltpu.VMEM((REPS, 4, PT), F32),
            pltpu.VMEM((STOPS, 4, PT), F32),
            pltpu.VMEM((STOPS, 4, PT), F32),
            pltpu.VMEM((REPS, PT, FEATURES), BF16),
            pltpu.VMEM((REPS, STOPS, PT, 2 * PT), BF16),
            pltpu.VMEM((STOPS, 32, 2 * PT), BF16),
            pltpu.VMEM((PT, 32), F32),
            pltpu.VMEM((REPS - 1, 4, PT), F32),
            pltpu.VMEM((REPS - 1, 4, PT), F32),
            pltpu.VMEM((CAP, SLOT_ROWS, LANES), I32),
            pltpu.VMEM((CAP, SLOT_ROWS, LANES), I32),
            pltpu.VMEM((BLOCKS, PT), BF16),
            dma((7,)), dma((8,)), dma((4,)), dma((REPS,)), dma((STOPS,)), dma((STOPS,)),
            dma((REPS - 1,)),
        ],
        compiler_params=pltpu.CompilerParams(
            collective_id=0, has_side_effects=True, vmem_limit_bytes=52 * 1024 * 1024
        ),
        cost_estimate=pl.CostEstimate(
            flops=2 * PT * SOURCES * PT * 128, bytes_accessed=1 << 20,
            transcendentals=PT * SOURCES * PT,
        ),
    )(
        positions,
        normal_flow,
        send_owner.reshape(1, PT),
        send_slot.reshape(1, PT),
        recv_index.reshape(CAP, BLOCKS),
        loop_pos.reshape(COLUMN_ROWS, LANES),
        loop_len.reshape(COLUMN_ROWS, LANES),
    )


def solution(mesh):
    both = P(("blk", "rep"))
    wide = P(None, ("blk", "rep"))
    return jax.shard_map(
        shards,
        mesh=mesh,
        in_specs=(wide, wide, both, both, both, both, both),
        out_specs=wide,
        check_vma=False,
    )
```

time: 66.5 us -> 63.6 us (0.956)
  Pallas kernels: 64.6 us -> 57.7 us
  local copies, waits for them, and re-layouts: 1.3 us -> 5.44 us
    pallas_call x1, Pallas kernels: 64.6 us -> 57.7 us  [shards(): pl.pallas_call(kernel, out_shape=jax.ShapeDtypeStruct((3, PT), F32), in_s...]
    unnamed x1 -> x15, local copies, waits for them, and re-layouts: 1.3 us -> 5.44 us
where the time goes in v2:
time: 63.6 us; the launch traced here: 63.1 us
  Pallas kernels  57.7 us (91%)
  local copies, waits for them, and re-layouts  5.44 us (9%)
    pallas_call x1, Pallas kernels, shards(): pl.pallas_call(kernel, out_shape=jax.ShapeDtypeStruct((3, PT), F32), in_s...  57.7 us
    unnamed x15, local copies, waits for them, and re-layouts  5.44 us

profile of v2, /device:TPU:1, one launch (start us, length us, event | category | flops | bytes accessed | tf_op | source)
XLA Modules:
  0.0 63.1 jit_solution(7290778158720550046)
XLA Ops:
  0.0 0.0 copy-start
  0.0 0.7 %copy-done = f32[3,512]{1,0:T(4,128)S(1)} copy-done((f32[3,512]{1,0:T(4,128)S(1)}, f32[3,512]{1,0:T(4,128)}, u32[]{:S(2)}) %copy-start) | copy-done | bytes 6168
  0.7 0.0 copy-start.1
  0.7 0.7 %copy-done.1 = f32[3,512]{1,0:T(4,128)S(1)} copy-done((f32[3,512]{1,0:T(4,128)S(1)}, f32[3,512]{1,0:T(4,128)}, u32[]{:S(2)}) %copy-start.1) | copy-done | bytes 6168
  1.4 0.0 copy-start.2
  1.4 0.7 %copy-done.2 = s32[1280]{0:T(1024)S(1)} copy-done((s32[1280]{0:T(1024)S(1)}, s32[1280]{0:T(1024)}, u32[]{:S(2)}) %copy-start.2) | copy-done | bytes 5144
  2.1 0.0 copy-start.3
  2.1 0.7 %copy-done.3 = s32[1280]{0:T(1024)S(1)} copy-done((s32[1280]{0:T(1024)S(1)}, s32[1280]{0:T(1024)}, u32[]{:S(2)}) %copy-start.3) | copy-done | bytes 5144
  2.8 0.0 copy-start.4
  2.8 0.7 %copy-done.4 = s32[1280]{0:T(1024)S(1)} copy-done((s32[1280]{0:T(1024)S(1)}, s32[1280]{0:T(1024)}, u32[]{:S(2)}) %copy-start.4) | copy-done | bytes 5144
  3.5 0.0 copy-start.5
  3.5 0.7 %copy-done.5 = s32[512]{0:T(512)S(1)} copy-done((s32[512]{0:T(512)S(1)}, s32[512]{0:T(512)}, u32[]{:S(2)}) %copy-start.5) | copy-done | bytes 2072
  4.2 0.0 copy-start.6
  4.2 0.7 %copy-done.6 = s32[512]{0:T(512)S(1)} copy-done((s32[512]{0:T(512)S(1)}, s32[512]{0:T(512)}, u32[]{:S(2)}) %copy-start.6) | copy-done | bytes 2072
  4.9 57.7 %shard_map.73 = f32[3,512]{1,0:T(4,128)S(1)} custom-call(f32[3,512]{1,0:T(4,128)S(1)} %copy-done, f32[3,512]{1,0:T(4,128)S(1)} %copy-done.1, s32[1,512]{1,0:T(1,128)S(1)} %bitcast.8, s32[1,512]{1,0:T(1,128)S(1)} %bitcast.9, s32[10,128]{1,0:T(8,128)S(1)} %bitcast.5, s32[10,128]{1,0:T(8,128)S(1)} %bitcast.6, s32[10,128]{1,0:T(8,128)S(1)} %bitcast.7), custom_call_target="tpu_custom_call" | custom-call | flops 2147483648 | bytes 1048576 | tf_op jit(solution)/shard_map/pallas_call | solution.py:396
  62.5 0.6 copy.9
Async XLA Ops:
  0.0 0.7 %copy-start = (f32[3,512]{1,0:T(4,128)S(1)}, f32[3,512]{1,0:T(4,128)}, u32[]{:S(2)}) copy-start(f32[3,512]{1,0:T(4,128)} %pos_hbm.1) | copy-start | bytes 18436
  0.7 0.7 %copy-start.1 = (f32[3,512]{1,0:T(4,128)S(1)}, f32[3,512]{1,0:T(4,128)}, u32[]{:S(2)}) copy-start(f32[3,512]{1,0:T(4,128)} %flow_hbm.1) | copy-start | bytes 18436
  1.4 0.7 %copy-start.2 = (s32[1280]{0:T(1024)S(1)}, s32[1280]{0:T(1024)}, u32[]{:S(2)}) copy-start(s32[1280]{0:T(1024)} %param.11) | copy-start | bytes 15364
  2.1 0.7 %copy-start.3 = (s32[1280]{0:T(1024)S(1)}, s32[1280]{0:T(1024)}, u32[]{:S(2)}) copy-start(s32[1280]{0:T(1024)} %param.12) | copy-start | bytes 15364
  2.8 0.7 %copy-start.4 = (s32[1280]{0:T(1024)S(1)}, s32[1280]{0:T(1024)}, u32[]{:S(2)}) copy-start(s32[1280]{0:T(1024)} %param.13) | copy-start | bytes 15364
  3.5 0.7 %copy-start.5 = (s32[512]{0:T(512)S(1)}, s32[512]{0:T(512)}, u32[]{:S(2)}) copy-start(s32[512]{0:T(512)} %param.9) | copy-start | bytes 6148
  4.2 0.7 %copy-start.6 = (s32[512]{0:T(512)S(1)}, s32[512]{0:T(512)}, u32[]{:S(2)}) copy-start(s32[512]{0:T(512)} %param.10) | copy-start | bytes 6148

commit v3 on v2

--- a/solution.py
+++ b/solution.py
@@ -28,7 +28,9 @@
 COLUMN_ROWS = 10
 
 FEATURES = 64
-STOP_ORDER = (0, 1, -1, 2, -2, 3, -3, 4)
+STOP_ORDER = (0, 4, 3, -3, 2, -2, 1, -1)
+LINE_ORDER = (4, 3, 5, 2, 6, 1, 7)
+PLANE_ORDER = (10, 9, 11, 6, 14, 7, 13, 2, 8, 5, 15, 3, 1, 4, 12)
 
 MESH = pl.DeviceIdType.MESH
 F32 = jnp.float32
@@ -87,7 +89,7 @@
     pos_hbm, flow_hbm, owner_hbm, slot_hbm, recv_hbm, order_hbm, count_hbm, out_ref,
     pos_ref, flow_ref, owner_ref, slot_ref, recv_ref, order_ref, count_ref,
     out1, in1, turned1, arrived, out2, in2, turned2, returned,
-    targets, src_pos, src_tan, target, weights, right, total, part_out, part_in,
+    targets, src_pos, src_tan, target, features, weights, right, total, part_out, part_in,
     index_a, index_b, member,
     load_sem, send_sem, phase_sem, rep_sem, pos_sem, tan_sem, part_sem,
 ):
@@ -113,9 +115,9 @@
     def greet(blk, other):
         pl.semaphore_signal(barrier, inc=1, device_id=(blk, other), device_id_type=MESH)
 
-    for k in range(1, LINE):
+    for k in LINE_ORDER:
         greet(plane * LINE + on_line(k), rep)
-    for k in range(1, PLANES):
+    for k in PLANE_ORDER:
         greet(on_plane(k) * LINE + place, rep)
     for k in range(1, REPS):
         greet(me, on_rep(k))
@@ -163,13 +165,13 @@
         ).start()
 
     def send_line(src, dst, phase):
-        for k in range(1, LINE):
+        for k in LINE_ORDER:
             there = on_line(k)
             copy_to(src.at[there], dst.at[place], phase, phase_sem.at[phase],
                     plane * LINE + there, rep)
 
     def send_plane(src, dst, phase):
-        for k in range(1, PLANES):
+        for k in PLANE_ORDER:
             there = on_plane(k)
             copy_to(src.at[there], dst.at[plane], phase, phase_sem.at[phase],
                     there * LINE + place, rep)
@@ -196,37 +198,43 @@
             [-2.0 * rows[0:3], ones, rows[3:4] + CORE_SQUARED, none], axis=0
         )
         th, tm, tl = split(wanted)
-        features = jnp.concatenate(
+        rows = jnp.concatenate(
             [th, th, tm, tm, th, tl, tl, tm, jnp.zeros((LANES - FEATURES, PT), F32)], axis=0
         )
-        target[other] = features.T[:, :FEATURES].astype(BF16)
-
-    def weigh(stop, reps):
+        target[other] = rows.T[:, :FEATURES].astype(BF16)
+
+    def describe(stop):
         sh, sm, sl = split(jnp.concatenate([src_pos[stop + BACK], one_row], axis=0))
-        rows = jnp.concatenate([sh, sm, sh, sm, sl, sh, sm, sl], axis=0).astype(BF16)
-        for k in reps:
+        features[...] = jnp.concatenate([sh, sm, sh, sm, sl, sh, sm, sl], axis=0).astype(BF16)
+
+    def weigh(stop, low, top):
+        def one(k, carry):
             other = on_rep(k)
             for half in range(PT // 256):
                 low, top = half * 256, half * 256 + 256
-                root = lax.rsqrt(dot(target[other], rows[:, low:top]))
+                root = lax.rsqrt(dot(target[other], features[:, low:top]))
                 weight = root * root * root
                 high = weight.astype(BF16)
                 weights[other, stop + BACK, :, low:top] = high
                 weights[other, stop + BACK, :, PT + low : PT + top] = (
                     weight - high.astype(F32)
                 ).astype(BF16)
+            return carry
+
+        lax.fori_loop(low, top, one, 0)
 
     def weigh_stops(low, top):
         def one(i, carry):
             stop = (i % 2) * ((i + 1) // 2) - (1 - i % 2) * (i // 2)
             await_here(src_pos.at[stop + BACK], pos_sem.at[stop + BACK])
-            weigh(stop, range(REPS))
+            describe(stop)
+            weigh(stop, 0, REPS)
             return carry
 
         lax.fori_loop(low, top, one, 0)
 
     aim(rep)
-    weigh(0, [0])
+    describe(0)
 
     pl.semaphore_wait(barrier, (LINE - 1) + (PLANES - 1) + (REPS - 1) + (STOPS - 1))
 
@@ -277,7 +285,7 @@
     for k in range(1, REPS):
         await_here(targets.at[on_rep(k)], rep_sem.at[on_rep(k)])
         aim(on_rep(k))
-    weigh(0, range(1, REPS))
+    weigh(0, 0, REPS)
 
     await_here(arrived.at[pl.ds(0, PLANES - 1)], phase_sem.at[1])
     tables = arrived[...].reshape(BLOCKS, LANES).T
@@ -349,16 +357,24 @@
         parts = total[...].T
         parts = parts[0:8] + parts[8:16] + parts[16:24]
         far = cross(rows_of(parts, 0, 3), rows_of(targets[other], 0, 3))
-        return [far[c] - parts[3 + c : 4 + c] for c in range(3)]
-
+        part_out[k % REPS] = jnp.concatenate(
+            [far[c] - parts[3 + c : 4 + c] for c in range(3)] + [jnp.zeros((1, PT), F32)], axis=0
+        )
+
+    def sums_of(k, carry):
+        gather_sums(k)
+
+        @pl.when(k < REPS)
+        def _():
+            copy_to(part_out.at[k], part_in.at[k], 7, part_sem.at[k], me, on_rep(k))
+
+        return carry
+
+    lax.fori_loop(1, REPS + 1, sums_of, 0)
     for k in range(1, REPS):
-        part_out[k - 1] = jnp.concatenate(gather_sums(k) + [jnp.zeros((1, PT), F32)], axis=0)
-        copy_to(part_out.at[k - 1], part_in.at[k - 1], 7, part_sem.at[k - 1], me, on_rep(k))
-    far = gather_sums(0)
-    for k in range(1, REPS):
-        await_here(part_in.at[k - 1], part_sem.at[k - 1])
-    others = part_in[0] + part_in[1] + part_in[2]
-    far = [far[c] + others[c : c + 1] for c in range(3)]
+        await_here(part_in.at[k], part_sem.at[k])
+    others = part_out[0] + part_in[1] + part_in[2] + part_in[3]
+    far = [others[c : c + 1] for c in range(3)]
 
     tangent, curvature = rows_of(derived, 0, 3), rows_of(derived, 3, 6)
     speed = jnp.maximum(
@@ -383,7 +399,7 @@
     await_sent(targets.at[pl.ds(0, REPS - 1)], 4)
     await_sent(src_pos.at[pl.ds(0, STOPS - 1)], 5)
     await_sent(src_tan.at[pl.ds(0, STOPS - 1)], 6)
-    await_sent(part_out, 7)
+    await_sent(part_out.at[pl.ds(1, REPS - 1)], 7)
 
 
 def shards(positions, normal_flow, send_owner, send_slot, recv_index, loop_pos, loop_len):
@@ -405,19 +421,20 @@
             pltpu.VMEM((STOPS, 4, PT), F32),
             pltpu.VMEM((STOPS, 4, PT), F32),
             pltpu.VMEM((REPS, PT, FEATURES), BF16),
+            pltpu.VMEM((FEATURES, PT), BF16),
             pltpu.VMEM((REPS, STOPS, PT, 2 * PT), BF16),
             pltpu.VMEM((STOPS, 32, 2 * PT), BF16),
             pltpu.VMEM((PT, 32), F32),
-            pltpu.VMEM((REPS - 1, 4, PT), F32),
-            pltpu.VMEM((REPS - 1, 4, PT), F32),
+            pltpu.VMEM((REPS, 4, PT), F32),
+            pltpu.VMEM((REPS, 4, PT), F32),
             pltpu.VMEM((CAP, SLOT_ROWS, LANES), I32),
             pltpu.VMEM((CAP, SLOT_ROWS, LANES), I32),
             pltpu.VMEM((BLOCKS, PT), BF16),
             dma((7,)), dma((8,)), dma((4,)), dma((REPS,)), dma((STOPS,)), dma((STOPS,)),
-            dma((REPS - 1,)),
+            dma((REPS,)),
         ],
         compiler_params=pltpu.CompilerParams(
-            collective_id=0, has_side_effects=True, vmem_limit_bytes=52 * 1024 * 1024
+            collective_id=0, has_side_effects=True, vmem_limit_bytes=60 * 1024 * 1024
         ),
         cost_estimate=pl.CostEstimate(
             flops=2 * PT * SOURCES * PT * 128, bytes_accessed=1 << 20,

time: 63.6 us -> 59.3 us (0.932)
  local copies, waits for them, and re-layouts: 5.44 us -> 1.3 us
    unnamed x15 -> x1, local copies, waits for them, and re-layouts: 5.44 us -> 1.3 us
where the time goes in v3:
time: 59.3 us; the launch traced here: 59.1 us
  Pallas kernels  57.8 us (97%)
  local copies, waits for them, and re-layouts  1.3 us (2%)
    pallas_call x1, Pallas kernels, shards(): pl.pallas_call(kernel, out_shape=jax.ShapeDtypeStruct((3, PT), F32), in_s...  57.8 us
    unnamed x1, local copies, waits for them, and re-layouts  1.3 us

profile of v3, /device:TPU:1, one launch (start us, length us, event | category | flops | bytes accessed | tf_op | source)
XLA Modules:
  0.0 59.1 jit_solution(12105302323610926766)
XLA Ops:
  0.0 57.8 %shard_map.73 = f32[3,512]{1,0:T(4,128)} custom-call(f32[3,512]{1,0:T(4,128)} %pos_hbm.1, f32[3,512]{1,0:T(4,128)} %flow_hbm.1, s32[1,512]{1,0:T(1,128)} %bitcast.8, s32[1,512]{1,0:T(1,128)} %bitcast.9, s32[10,128]{1,0:T(8,128)} %bitcast.5, s32[10,128]{1,0:T(8,128)} %bitcast.6, s32[10,128]{1,0:T(8,128)} %bitcast.7), custom_call_target="tpu_custom_call" | custom-call | flops 2147483648 | bytes 1048576 | tf_op jit(solution)/shard_map/pallas_call | solution.py:412
  57.8 1.3 %copy.9 = f32[3,512]{1,0:T(4,128)} copy(f32[3,512]{1,0:T(4,128)} %shard_map.73) | data formatting | bytes 12288

commit v4 on v3

--- a/solution.py
+++ b/solution.py
@@ -89,7 +89,7 @@
     pos_hbm, flow_hbm, owner_hbm, slot_hbm, recv_hbm, order_hbm, count_hbm, out_ref,
     pos_ref, flow_ref, owner_ref, slot_ref, recv_ref, order_ref, count_ref,
     out1, in1, turned1, arrived, out2, in2, turned2, returned,
-    targets, src_pos, src_tan, target, features, weights, right, total, part_out, part_in,
+    targets, src_pos, src_tan, target, features, weights, right, part_out, part_in,
     index_a, index_b, member,
     load_sem, send_sem, phase_sem, rep_sem, pos_sem, tan_sem, part_sem,
 ):
@@ -109,20 +109,6 @@
 
     def block(stop):
         return (me + stop + BLOCKS) % BLOCKS
-
-    barrier = pltpu.get_barrier_semaphore()
-
-    def greet(blk, other):
-        pl.semaphore_signal(barrier, inc=1, device_id=(blk, other), device_id_type=MESH)
-
-    for k in LINE_ORDER:
-        greet(plane * LINE + on_line(k), rep)
-    for k in PLANE_ORDER:
-        greet(on_plane(k) * LINE + place, rep)
-    for k in range(1, REPS):
-        greet(me, on_rep(k))
-    for stop in STOP_ORDER[1:]:
-        greet(block(stop), rep)
 
     loads = [
         pltpu.make_async_copy(src, dst, load_sem.at[i])
@@ -134,7 +120,24 @@
             ]
         )
     ]
-    for load in loads:
+    for load in loads[:3]:
+        load.start()
+
+    barrier = pltpu.get_barrier_semaphore()
+
+    def greet(blk, other):
+        pl.semaphore_signal(barrier, inc=1, device_id=(blk, other), device_id_type=MESH)
+
+    for k in LINE_ORDER:
+        greet(plane * LINE + on_line(k), rep)
+    for k in PLANE_ORDER:
+        greet(on_plane(k) * LINE + place, rep)
+    for k in range(1, REPS):
+        greet(me, on_rep(k))
+    for stop in STOP_ORDER[1:]:
+        greet(block(stop), rep)
+
+    for load in loads[3:]:
         load.start()
     for load in loads[:3]:
         load.wait()
@@ -198,25 +201,25 @@
             [-2.0 * rows[0:3], ones, rows[3:4] + CORE_SQUARED, none], axis=0
         )
         th, tm, tl = split(wanted)
-        rows = jnp.concatenate(
-            [th, th, tm, tm, th, tl, tl, tm, jnp.zeros((LANES - FEATURES, PT), F32)], axis=0
-        )
-        target[other] = rows.T[:, :FEATURES].astype(BF16)
+        target[other] = jnp.concatenate([th, th, tm, tm, th, tl, tl, tm], axis=0).astype(BF16)
 
     def describe(stop):
         sh, sm, sl = split(jnp.concatenate([src_pos[stop + BACK], one_row], axis=0))
-        features[...] = jnp.concatenate([sh, sm, sh, sm, sl, sh, sm, sl], axis=0).astype(BF16)
+        rows = jnp.concatenate(
+            [sh, sm, sh, sm, sl, sh, sm, sl, jnp.zeros((LANES - FEATURES, PT), F32)], axis=0
+        )
+        features[...] = rows.T[:, :FEATURES].astype(BF16)
 
     def weigh(stop, low, top):
         def one(k, carry):
             other = on_rep(k)
             for half in range(PT // 256):
                 low, top = half * 256, half * 256 + 256
-                root = lax.rsqrt(dot(target[other], features[:, low:top]))
+                root = lax.rsqrt(dot(features[...], target[other, :, low:top]))
                 weight = root * root * root
                 high = weight.astype(BF16)
-                weights[other, stop + BACK, :, low:top] = high
-                weights[other, stop + BACK, :, PT + low : PT + top] = (
+                weights[other, stop + BACK, :PT, low:top] = high
+                weights[other, stop + BACK, PT:, low:top] = (
                     weight - high.astype(F32)
                 ).astype(BF16)
             return carry
@@ -233,17 +236,12 @@
 
         lax.fori_loop(low, top, one, 0)
 
-    aim(rep)
-    describe(0)
 
     pl.semaphore_wait(barrier, (LINE - 1) + (PLANES - 1) + (REPS - 1) + (STOPS - 1))
 
     send_line(out1, in1, 0)
     for k in range(1, REPS):
         copy_to(targets.at[rep], targets.at[rep], 4, rep_sem.at[rep], me, on_rep(k))
-    for stop in STOP_ORDER[1:]:
-        copy_to(src_pos.at[BACK], src_pos.at[stop + BACK], 5, pos_sem.at[stop + BACK],
-                block(-stop), rep)
     in1[place] = out1[place]
 
     for load in loads[3:]:
@@ -271,11 +269,16 @@
         there = jnp.clip(at - order + moved, 0, COLUMN_ROWS * LANES - 1)
         return look_up(inverse, there)
 
+    aim(rep)
+    describe(0)
     await_here(in1.at[pl.ds(0, LINE - 1)], phase_sem.at[0])
     for j in range(PLANES):
         turned1[j] = in1[:, j, :]
     send_plane(turned1, arrived, 1)
     arrived[plane] = turned1[plane]
+    for stop in STOP_ORDER[1:]:
+        copy_to(src_pos.at[BACK], src_pos.at[stop + BACK], 5, pos_sem.at[stop + BACK],
+                block(-stop), rep)
 
     ahead1, ahead2, behind1, behind2 = (neighbour(k) for k in (1, 2, -1, -2))
     near = iota((SLOT_ROWS, LANES), 0) < 3
@@ -345,16 +348,13 @@
 
     def gather_sums(k):
         other = on_rep(k)
-        total[...] = jnp.zeros_like(total)
-
-        def one(i, carry):
-            total[...] += dot(weights[other, 2 * i], right[2 * i], NT) + dot(
-                weights[other, 2 * i + 1], right[2 * i + 1], NT
-            )
-            return carry
-
-        lax.fori_loop(0, STOPS // 2, one, 0)
-        parts = total[...].T
+
+        def some(i, sums):
+            for j in range(4):
+                sums = sums + dot(right[4 * i + j], weights[other, 4 * i + j])
+            return sums
+
+        parts = lax.fori_loop(0, STOPS // 4, some, jnp.zeros((32, PT), F32))
         parts = parts[0:8] + parts[8:16] + parts[16:24]
         far = cross(rows_of(parts, 0, 3), rows_of(targets[other], 0, 3))
         part_out[k % REPS] = jnp.concatenate(
@@ -420,11 +420,10 @@
             pltpu.VMEM((REPS, 4, PT), F32),
             pltpu.VMEM((STOPS, 4, PT), F32),
             pltpu.VMEM((STOPS, 4, PT), F32),
-            pltpu.VMEM((REPS, PT, FEATURES), BF16),
-            pltpu.VMEM((FEATURES, PT), BF16),
-            pltpu.VMEM((REPS, STOPS, PT, 2 * PT), BF16),
+            pltpu.VMEM((REPS, FEATURES, PT), BF16),
+            pltpu.VMEM((PT, FEATURES), BF16),
+            pltpu.VMEM((REPS, STOPS, 2 * PT, PT), BF16),
             pltpu.VMEM((STOPS, 32, 2 * PT), BF16),
-            pltpu.VMEM((PT, 32), F32),
             pltpu.VMEM((REPS, 4, PT), F32),
             pltpu.VMEM((REPS, 4, PT), F32),
             pltpu.VMEM((CAP, SLOT_ROWS, LANES), I32),

time: 59.3 us -> 55.7 us (0.939)
  Pallas kernels: 57.8 us -> 54.1 us
    pallas_call x1, Pallas kernels: 57.8 us -> 54.1 us  [shards(): pl.pallas_call(kernel, out_shape=jax.ShapeDtypeStruct((3, PT), F32), in_s...]
where the time goes in v4:
time: 55.7 us; the launch traced here: 55.4 us
  Pallas kernels  54.1 us (97%)
  local copies, waits for them, and re-layouts  1.3 us (2%)
    pallas_call x1, Pallas kernels, shards(): pl.pallas_call(kernel, out_shape=jax.ShapeDtypeStruct((3, PT), F32), in_s...  54.1 us
    unnamed x1, local copies, waits for them, and re-layouts  1.3 us

profile of v4, /device:TPU:1, one launch (start us, length us, event | category | flops | bytes accessed | tf_op | source)
XLA Modules:
  0.0 55.4 jit_solution(7629887978107876473)
XLA Ops:
  0.0 54.1 %shard_map.73 = f32[3,512]{1,0:T(4,128)} custom-call(f32[3,512]{1,0:T(4,128)} %pos_hbm.1, f32[3,512]{1,0:T(4,128)} %flow_hbm.1, s32[1,512]{1,0:T(1,128)} %bitcast.8, s32[1,512]{1,0:T(1,128)} %bitcast.9, s32[10,128]{1,0:T(8,128)} %bitcast.5, s32[10,128]{1,0:T(8,128)} %bitcast.6, s32[10,128]{1,0:T(8,128)} %bitcast.7), custom_call_target="tpu_custom_call" | custom-call | flops 2147483648 | bytes 1048576 | tf_op jit(solution)/shard_map/pallas_call | solution.py:412
  54.2 1.3 %copy.9 = f32[3,512]{1,0:T(4,128)} copy(f32[3,512]{1,0:T(4,128)} %shard_map.73) | data formatting | bytes 12288

commit v5 on v4

--- a/solution.py
+++ b/solution.py
@@ -30,6 +30,7 @@
 FEATURES = 64
 STOP_ORDER = (0, 4, 3, -3, 2, -2, 1, -1)
 LINE_ORDER = (4, 3, 5, 2, 6, 1, 7)
+LATE = 6
 PLANE_ORDER = (10, 9, 11, 6, 14, 7, 13, 2, 8, 5, 15, 3, 1, 4, 12)
 
 MESH = pl.DeviceIdType.MESH
@@ -91,7 +92,7 @@
     out1, in1, turned1, arrived, out2, in2, turned2, returned,
     targets, src_pos, src_tan, target, features, weights, right, part_out, part_in,
     index_a, index_b, member,
-    load_sem, send_sem, phase_sem, rep_sem, pos_sem, tan_sem, part_sem,
+    load_sem, ready, send_sem, phase_sem, rep_sem, pos_sem, tan_sem, part_sem,
 ):
     me = lax.axis_index("blk")
     rep = lax.axis_index("rep")
@@ -128,21 +129,75 @@
     def greet(blk, other):
         pl.semaphore_signal(barrier, inc=1, device_id=(blk, other), device_id_type=MESH)
 
-    for k in LINE_ORDER:
-        greet(plane * LINE + on_line(k), rep)
-    for k in PLANE_ORDER:
-        greet(on_plane(k) * LINE + place, rep)
-    for k in range(1, REPS):
-        greet(me, on_rep(k))
-    for stop in STOP_ORDER[1:]:
-        greet(block(stop), rep)
+    def loop(low, top, act):
+        def one(i, carry):
+            act(i)
+            return carry
+
+        lax.fori_loop(low, top, one, 0)
+
+    def step_in(t):
+        return (t - place + BACK + LINE) % LINE - BACK
+
+    def step_out(t):
+        return (t - place + BACK + 1 + LINE) % LINE - BACK - 1
+
+    def greet_block(t):
+        greet(block(step_in(t)), rep)
+
+        @pl.when(t - place == STOPS // 2)
+        def _():
+            greet(block(-STOPS // 2), rep)
+
+    loop(place + 1, LINE, lambda t: greet(plane * LINE + t, rep))
+    loop(place + 1, LINE, greet_block)
+    loop(plane + 1, PLANES, lambda t: greet(t * LINE + place, rep))
+    loop(rep + 1, REPS, lambda t: greet(me, t))
 
     for load in loads[3:]:
         load.start()
+    lower = 2 * place + place // (STOPS // 2) + plane + rep
+
+    @pl.when(lower > 0)
+    def _():
+        pl.semaphore_wait(barrier, lower)
+
+    def accept(kind, blk):
+        pl.semaphore_signal(
+            ready.at[kind], inc=1, device_id=(blk, rep), device_id_type=MESH
+        )
+
+    loop(0, place, lambda t: accept(0, plane * LINE + t))
+    loop(0, plane, lambda t: accept(1, t * LINE + place))
+
+    @pl.when(place >= STOPS // 2)
+    def _():
+        accept(2, block(STOPS // 2))
+
     for load in loads[:3]:
         load.wait()
 
+    def copy_to(src, dst, send, recv, blk, other):
+        pltpu.make_async_remote_copy(
+            src_ref=src, dst_ref=dst, send_sem=send_sem.at[send], recv_sem=recv,
+            device_id=(blk, other), device_id_type=MESH,
+        ).start()
+
+    def send_pos(t):
+        step = step_out(t)
+        copy_to(src_pos.at[BACK], src_pos.at[BACK - step], 5, pos_sem.at[BACK - step],
+                block(step), rep)
+
+    def send_target(t):
+        copy_to(targets.at[rep], targets.at[rep], 4, rep_sem.at[rep], me, t)
+
     pos = pos_ref[...]
+    square = jnp.sum(pos * pos, axis=0, keepdims=True)
+    pos_rows = jnp.concatenate([pos, square], axis=0)
+    src_pos[BACK] = pos_rows
+    targets[rep] = pos_rows
+    loop(0, place, send_pos)
+    loop(0, rep, send_target)
     owner = owner_ref[...]
     slot = slot_ref[...]
     owner_row = (owner & (LINE - 1)) * PLANES + (owner >> 3)
@@ -156,17 +211,6 @@
     )
     outgoing = sum(dot(is_owner, part.astype(BF16), NT) for part in split(slotted))
     out1[...] = outgoing.reshape(LINE, PLANES, LANES)
-    square = jnp.sum(pos * pos, axis=0, keepdims=True)
-    pos_rows = jnp.concatenate([pos, square], axis=0)
-    src_pos[BACK] = pos_rows
-    targets[rep] = pos_rows
-
-    def copy_to(src, dst, send, recv, blk, other):
-        pltpu.make_async_remote_copy(
-            src_ref=src, dst_ref=dst, send_sem=send_sem.at[send], recv_sem=recv,
-            device_id=(blk, other), device_id_type=MESH,
-        ).start()
-
     def send_line(src, dst, phase):
         for k in LINE_ORDER:
             there = on_line(k)
@@ -210,9 +254,11 @@
         )
         features[...] = rows.T[:, :FEATURES].astype(BF16)
 
-    def weigh(stop, low, top):
-        def one(k, carry):
-            other = on_rep(k)
+    def weigh(t):
+        stop = step_in(t)
+        describe(stop)
+
+        def one(other):
             for half in range(PT // 256):
                 low, top = half * 256, half * 256 + 256
                 root = lax.rsqrt(dot(features[...], target[other, :, low:top]))
@@ -222,26 +268,77 @@
                 weights[other, stop + BACK, PT:, low:top] = (
                     weight - high.astype(F32)
                 ).astype(BF16)
-            return carry
-
-        lax.fori_loop(low, top, one, 0)
-
-    def weigh_stops(low, top):
-        def one(i, carry):
-            stop = (i % 2) * ((i + 1) // 2) - (1 - i % 2) * (i // 2)
-            await_here(src_pos.at[stop + BACK], pos_sem.at[stop + BACK])
-            describe(stop)
-            weigh(stop, 0, REPS)
-            return carry
-
-        lax.fori_loop(low, top, one, 0)
-
-
-    pl.semaphore_wait(barrier, (LINE - 1) + (PLANES - 1) + (REPS - 1) + (STOPS - 1))
+
+        loop(0, REPS, one)
+
+    def await_pos(t):
+        await_here(src_pos.at[step_in(t) + BACK], pos_sem.at[step_in(t) + BACK])
+
+    def higher_reps():
+        def one(t):
+            await_here(targets.at[t], rep_sem.at[t])
+            send_target(t)
+
+        loop(rep + 1, REPS, one)
+
+    def lower_reps():
+        loop(0, rep, lambda t: await_here(targets.at[t], rep_sem.at[t]))
+        loop(0, REPS, aim)
+
+    early = place < LATE
+    low_count = jnp.where(place < 2, place, jnp.where(place < 3, 2, jnp.where(early, 5 - place, 0)))
+    high_top = jnp.where(place < 3, 5 - place, place)
+
+    def in_turn(i):
+        return jnp.where(i == 0, place, jnp.where(i <= place, i - 1, i))
+
+    def is_early(t):
+        return early & jnp.where(t == place, True, jnp.where(t < place, t < low_count, t <= high_top))
+
+    def serve(i):
+        t = in_turn(i)
+
+        @pl.when(t > place)
+        def _():
+            await_pos(t)
+
+            @pl.when(t - place == STOPS // 2)
+            def _():
+                pl.semaphore_wait(ready.at[2], 1)
+
+            send_pos(t)
+
+        @pl.when(is_early(t))
+        def _():
+            @pl.when(t < place)
+            def _():
+                await_pos(t)
+
+            weigh(t)
+
+    def finish(i):
+        t = in_turn(i)
+
+        @pl.when(jnp.logical_not(is_early(t) | (early & (t >= LATE))))
+        def _():
+            @pl.when(t < place)
+            def _():
+                await_pos(t)
+
+            weigh(t)
+
+    @pl.when(early)
+    def _():
+        higher_reps()
+        lower_reps()
+
+    loop(0, LINE, serve)
+
+    @pl.when(place < LINE - 1)
+    def _():
+        pl.semaphore_wait(ready.at[0], LINE - 1 - place)
 
     send_line(out1, in1, 0)
-    for k in range(1, REPS):
-        copy_to(targets.at[rep], targets.at[rep], 4, rep_sem.at[rep], me, on_rep(k))
     in1[place] = out1[place]
 
     for load in loads[3:]:
@@ -269,27 +366,22 @@
         there = jnp.clip(at - order + moved, 0, COLUMN_ROWS * LANES - 1)
         return look_up(inverse, there)
 
-    aim(rep)
-    describe(0)
     await_here(in1.at[pl.ds(0, LINE - 1)], phase_sem.at[0])
     for j in range(PLANES):
         turned1[j] = in1[:, j, :]
+
+    @pl.when(plane < PLANES - 1)
+    def _():
+        pl.semaphore_wait(ready.at[1], PLANES - 1 - plane)
+
     send_plane(turned1, arrived, 1)
     arrived[plane] = turned1[plane]
-    for stop in STOP_ORDER[1:]:
-        copy_to(src_pos.at[BACK], src_pos.at[stop + BACK], 5, pos_sem.at[stop + BACK],
-                block(-stop), rep)
 
     ahead1, ahead2, behind1, behind2 = (neighbour(k) for k in (1, 2, -1, -2))
     near = iota((SLOT_ROWS, LANES), 0) < 3
     for s in range(CAP):
         index_a[s] = jnp.where(near, ahead1[s : s + 1], ahead2[s : s + 1])
         index_b[s] = jnp.where(near, behind1[s : s + 1], behind2[s : s + 1])
-    for k in range(1, REPS):
-        await_here(targets.at[on_rep(k)], rep_sem.at[on_rep(k)])
-        aim(on_rep(k))
-    weigh(0, 0, REPS)
-
     await_here(arrived.at[pl.ds(0, PLANES - 1)], phase_sem.at[1])
     tables = arrived[...].reshape(BLOCKS, LANES).T
     middle = iota((SLOT_ROWS, LANES), 0) < 6
@@ -313,13 +405,25 @@
 
     send_plane(out2, in2, 2)
     in2[plane] = out2[plane]
-    weigh_stops(1, 3)
+
+    @pl.when(early)
+    def _():
+        weigh(LATE)
+
+    @pl.when(jnp.logical_not(early))
+    def _():
+        higher_reps()
+
     await_here(in2.at[pl.ds(0, PLANES - 1)], phase_sem.at[2])
     for j in range(LINE):
         turned2[j] = in2[:, j, :]
     send_line(turned2, returned, 3)
     returned[place] = turned2[place]
-    weigh_stops(3, 5)
+
+    @pl.when(early)
+    def _():
+        weigh(LATE + 1)
+
     await_here(returned.at[pl.ds(0, LINE - 1)], phase_sem.at[3])
     back = returned[...].reshape(BLOCKS, LANES).T
     is_owner = member[...]
@@ -332,7 +436,12 @@
     for stop in STOP_ORDER[1:]:
         copy_to(src_tan.at[BACK], src_tan.at[stop + BACK], 6, tan_sem.at[stop + BACK],
                 block(-stop), rep)
-    weigh_stops(5, STOPS)
+
+    @pl.when(jnp.logical_not(early))
+    def _():
+        lower_reps()
+
+    loop(0, LINE, finish)
 
     def prepare(stop):
         p, t = rows_of(src_pos[stop], 0, 3), rows_of(src_tan[stop], 0, 3)
@@ -429,7 +538,7 @@
             pltpu.VMEM((CAP, SLOT_ROWS, LANES), I32),
             pltpu.VMEM((CAP, SLOT_ROWS, LANES), I32),
             pltpu.VMEM((BLOCKS, PT), BF16),
-            dma((7,)), dma((8,)), dma((4,)), dma((REPS,)), dma((STOPS,)), dma((STOPS,)),
+            dma((7,)), pltpu.SemaphoreType.REGULAR((3,)), dma((8,)), dma((4,)), dma((REPS,)), dma((STOPS,)), dma((STOPS,)),
             dma((REPS,)),
         ],
         compiler_params=pltpu.CompilerParams(

time: 55.7 us -> 74.8 us (1.34)
  Pallas kernels: 54.1 us -> 73.3 us
    pallas_call x1, Pallas kernels: 54.1 us -> 73.3 us  [shards(): pl.pallas_call(kernel, out_shape=jax.ShapeDtypeStruct((3, PT), F32), in_s...]
where the time goes in v5:
time: 74.8 us; the launch traced here: 74.6 us
  Pallas kernels  73.3 us (98%)
  local copies, waits for them, and re-layouts  1.3 us (2%)
    pallas_call x1, Pallas kernels, shards(): pl.pallas_call(kernel, out_shape=jax.ShapeDtypeStruct((3, PT), F32), in_s...  73.3 us

profile of v5, /device:TPU:1, one launch (start us, length us, event | category | flops | bytes accessed | tf_op | source)
XLA Modules:
  0.0 74.6 jit_solution(4069111439776086970)
XLA Ops:
  0.0 73.3 %shard_map.73 = f32[3,512]{1,0:T(4,128)} custom-call(f32[3,512]{1,0:T(4,128)} %pos_hbm.1, f32[3,512]{1,0:T(4,128)} %flow_hbm.1, s32[1,512]{1,0:T(1,128)} %bitcast.8, s32[1,512]{1,0:T(1,128)} %bitcast.9, s32[10,128]{1,0:T(8,128)} %bitcast.5, s32[10,128]{1,0:T(8,128)} %bitcast.6, s32[10,128]{1,0:T(8,128)} %bitcast.7), custom_call_target="tpu_custom_call" | custom-call | flops 2147483648 | bytes 1048576 | tf_op jit(solution)/shard_map/pallas_call | solution.py:521
  73.3 1.3 %copy.9 = f32[3,512]{1,0:T(4,128)} copy(f32[3,512]{1,0:T(4,128)} %shard_map.73) | data formatting | bytes 12288

commit v6 on v4

--- a/solution.py
+++ b/solution.py
@@ -24,7 +24,6 @@
 PT = 512
 CAP = 10
 LANES = 128
-SLOT_ROWS = 8
 COLUMN_ROWS = 10
 
 FEATURES = 64
@@ -90,7 +89,7 @@
     pos_ref, flow_ref, owner_ref, slot_ref, recv_ref, order_ref, count_ref,
     out1, in1, turned1, arrived, out2, in2, turned2, returned,
     targets, src_pos, src_tan, target, features, weights, right, part_out, part_in,
-    index_a, index_b, member,
+    index, member,
     load_sem, send_sem, phase_sem, rep_sem, pos_sem, tan_sem, part_sem,
 ):
     me = lax.axis_index("blk")
@@ -145,17 +144,19 @@
     pos = pos_ref[...]
     owner = owner_ref[...]
     slot = slot_ref[...]
-    owner_row = (owner & (LINE - 1)) * PLANES + (owner >> 3)
-    is_owner = jnp.where(iota((BLOCKS, PT), 0) == owner_row, 1.0, 0.0).astype(BF16)
-    member[...] = is_owner
-    pos_twice = jnp.concatenate([pos, pos, jnp.zeros((2, PT), F32)], axis=0)
-    slotted = jnp.concatenate(
-        [jnp.where(slot == s, pos_twice, 0.0) for s in range(CAP)]
-        + [jnp.zeros((LANES - CAP * SLOT_ROWS, PT), F32)],
-        axis=0,
-    )
-    outgoing = sum(dot(is_owner, part.astype(BF16), NT) for part in split(slotted))
-    out1[...] = outgoing.reshape(LINE, PLANES, LANES)
+    owner_place, owner_plane = owner & (LINE - 1), owner >> 3
+    member_row = (owner_plane >> 3) * 64 + owner_place * 8 + (owner_plane & 7)
+    member[...] = jnp.where(iota((BLOCKS, PT), 0) == member_row, 1.0, 0.0).astype(BF16)
+    message_row = owner_place * 4 + (owner_plane >> 2)
+    to_row = jnp.where(iota((32, PT), 0) == message_row, 1.0, 0.0).astype(BF16)
+    lane = iota((LANES, PT), 0)
+    value = lane & 31
+    component = jnp.where(value < CAP, 0, jnp.where(value < 2 * CAP, 1, 2))
+    here = (lane >> 5) * 16 + value - component * CAP == (owner_plane & 3) * 16 + slot
+    slotted = jnp.where(component == 0, pos[0:1], jnp.where(component == 1, pos[1:2], pos[2:3]))
+    slotted = jnp.where(here, slotted, 0.0)
+    outgoing = sum(dot(to_row, part.astype(BF16), NT) for part in split(slotted))
+    out1[...] = outgoing.reshape(LINE, PLANES // 4, LANES)
     square = jnp.sum(pos * pos, axis=0, keepdims=True)
     pos_rows = jnp.concatenate([pos, square], axis=0)
     src_pos[BACK] = pos_rows
@@ -246,7 +247,8 @@
 
     for load in loads[3:]:
         load.wait()
-    spot = iota((16, LANES), 1) * CAP + iota((16, LANES), 0)
+    lane = iota((16, LANES), 1)
+    spot = (((lane & 31) >> 1) * LINE + (lane >> 5) * 2 + (lane & 1)) * CAP + iota((16, LANES), 0)
     column = jnp.where(iota((16, LANES), 0) < CAP, look_up(recv_ref[...], spot), -1)
     column_row, column_lane = column >> 7, column & 127
     holder = iota((16, LANES), 1).astype(F32)
@@ -272,8 +274,18 @@
     aim(rep)
     describe(0)
     await_here(in1.at[pl.ds(0, LINE - 1)], phase_sem.at[0])
-    for j in range(PLANES):
-        turned1[j] = in1[:, j, :]
+    place_bits, plane_bits = iota((LINE, LANES), 0) >> 1, iota((LINE, LANES), 1) >> 5
+    for q in range(PLANES // 4):
+        rows = in1[:, q, :]
+        down = pltpu.roll(pltpu.roll(rows, LINE - 2, 0), 32, 1)
+        up = pltpu.roll(pltpu.roll(rows, 2, 0), LANES - 32, 1)
+        rows = jnp.where(
+            (place_bits & 1) == (plane_bits & 1), rows, jnp.where((place_bits & 1) == 0, down, up)
+        )
+        far_rows = pltpu.roll(pltpu.roll(rows, 4, 0), 64, 1)
+        rows = jnp.where((place_bits >> 1) == (plane_bits >> 1), rows, far_rows)
+        for p in range(4):
+            turned1[4 * q + p] = rows[2 * p : 2 * p + 2]
     send_plane(turned1, arrived, 1)
     arrived[plane] = turned1[plane]
     for stop in STOP_ORDER[1:]:
@@ -281,54 +293,66 @@
                 block(-stop), rep)
 
     ahead1, ahead2, behind1, behind2 = (neighbour(k) for k in (1, 2, -1, -2))
-    near = iota((SLOT_ROWS, LANES), 0) < 3
-    for s in range(CAP):
-        index_a[s] = jnp.where(near, ahead1[s : s + 1], ahead2[s : s + 1])
-        index_b[s] = jnp.where(near, behind1[s : s + 1], behind2[s : s + 1])
+    for i, table in enumerate((ahead1, ahead2, behind1, behind2)):
+        index[i] = table
     for k in range(1, REPS):
         await_here(targets.at[on_rep(k)], rep_sem.at[on_rep(k)])
         aim(on_rep(k))
     weigh(0, 0, REPS)
 
     await_here(arrived.at[pl.ds(0, PLANES - 1)], phase_sem.at[1])
-    tables = arrived[...].reshape(BLOCKS, LANES).T
-    middle = iota((SLOT_ROWS, LANES), 0) < 6
-    results = []
-    for s in range(CAP):
-        to_a, to_b = index_a[s], index_b[s]
-        row_a, row_b, lane_a, lane_b = to_a >> 7, to_b >> 7, to_a & 127, to_b & 127
-        after = jnp.zeros((SLOT_ROWS, LANES), F32)
-        before = jnp.zeros((SLOT_ROWS, LANES), F32)
+    rows = arrived[...].reshape(2 * PLANES, LANES)
+    tables = jnp.concatenate(
+        [rows] + [pltpu.roll(rows, LANES - 32 * i, 1) for i in range(1, 4)], axis=0
+    ).T
+    moved = []
+    for i in range(4):
+        at_row, at_lane = index[i] >> 7, index[i] & 127
+        found = [jnp.zeros((16, LANES), F32) for _ in range(3)]
         for t in range(CAP):
-            table = tables[t * SLOT_ROWS : (t + 1) * SLOT_ROWS]
-            after = jnp.where(row_a == t, pick(table, lane_a), after)
-            before = jnp.where(row_b == t, pick(table, lane_b), before)
-        here = tables[s * SLOT_ROWS : (s + 1) * SLOT_ROWS]
-        gap, both = after - before, after + before
-        first = 8.0 * gap - pltpu.roll(gap, SLOT_ROWS - 3, 0)
-        second = 16.0 * pltpu.roll(both, 3, 0) - both - 30.0 * here
-        results.append(jnp.where(near, first, jnp.where(middle, second, 0.0)) / 12.0)
-    results.append(jnp.zeros((LANES - CAP * SLOT_ROWS, LANES), F32))
-    out2[...] = jnp.concatenate(results, axis=0).T.reshape(PLANES, LINE, LANES)
+            hit = at_row == t
+            for c in range(3):
+                table = jnp.broadcast_to(tables[c * CAP + t : c * CAP + t + 1], (16, LANES))
+                found[c] = jnp.where(hit, pick(table, at_lane), found[c])
+        moved.append(found)
+    results = [[], []]
+    for c in range(3):
+        a1, a2, b1, b2 = (found[c][:CAP] for found in moved)
+        center = tables[c * CAP : (c + 1) * CAP]
+        results[0].append((8.0 * (a1 - b1) - (a2 - b2)) / 12.0)
+        results[1].append((16.0 * (a1 + b1) - (a2 + b2) - 30.0 * center) / 12.0)
+    values = jnp.concatenate(
+        results[0] + results[1] + [jnp.zeros((64 - 6 * CAP, LANES), F32)], axis=0
+    )
+    values = jnp.concatenate([values, pltpu.roll(values, 64, 1)], axis=0).T
+    for i in range(2):
+        out2[:, i] = values[32 * i : 32 * i + 32].reshape(PLANES, 2, LANES)
 
     send_plane(out2, in2, 2)
     in2[plane] = out2[plane]
     weigh_stops(1, 3)
     await_here(in2.at[pl.ds(0, PLANES - 1)], phase_sem.at[2])
-    for j in range(LINE):
-        turned2[j] = in2[:, j, :]
+    left_half = iota((8, LANES), 1) < 64
+    for i in range(2):
+        for j in range(2):
+            rows = in2[:, i, j, :]
+            a, b = rows[:8], rows[8:]
+            turned2[2 * i + j] = jnp.where(left_half, a, pltpu.roll(b, 64, 1))
+            turned2[4 + 2 * i + j] = jnp.where(left_half, pltpu.roll(a, 64, 1), b)
     send_line(turned2, returned, 3)
     returned[place] = turned2[place]
     weigh_stops(3, 5)
     await_here(returned.at[pl.ds(0, LINE - 1)], phase_sem.at[3])
-    back = returned[...].reshape(BLOCKS, LANES).T
+    rows = returned[...].reshape(64, LANES)
+    back = jnp.concatenate([rows, pltpu.roll(rows, 64, 1)], axis=0).T[:64]
     is_owner = member[...]
     spread = sum(dot(part.astype(BF16), is_owner) for part in split(back))
-    derived = jnp.zeros((SLOT_ROWS, PT), F32)
-    for s in range(CAP):
-        derived = jnp.where(slot == s, spread[s * SLOT_ROWS : (s + 1) * SLOT_ROWS], derived)
-
-    src_tan[BACK] = jnp.concatenate([derived[0:3], jnp.zeros((1, PT), F32)], axis=0)
+    derived = []
+    for q in range(6):
+        chosen = jnp.where(iota((CAP, PT), 0) == slot, spread[q * CAP : (q + 1) * CAP], 0.0)
+        derived.append(jnp.sum(chosen, axis=0, keepdims=True))
+
+    src_tan[BACK] = jnp.concatenate(derived[0:3] + [jnp.zeros((1, PT), F32)], axis=0)
     for stop in STOP_ORDER[1:]:
         copy_to(src_tan.at[BACK], src_tan.at[stop + BACK], 6, tan_sem.at[stop + BACK],
                 block(-stop), rep)
@@ -376,7 +400,7 @@
     others = part_out[0] + part_in[1] + part_in[2] + part_in[3]
     far = [others[c : c + 1] for c in range(3)]
 
-    tangent, curvature = rows_of(derived, 0, 3), rows_of(derived, 3, 6)
+    tangent, curvature = derived[0:3], derived[3:6]
     speed = jnp.maximum(
         tangent[0] * tangent[0] + tangent[1] * tangent[1] + tangent[2] * tangent[2], SPEED_FLOOR
     )
@@ -404,8 +428,10 @@
 
 def shards(positions, normal_flow, send_owner, send_slot, recv_index, loop_pos, loop_len):
     dma = pltpu.SemaphoreType.DMA
-    by_line = pltpu.VMEM((LINE, PLANES, LANES), F32)
-    by_plane = pltpu.VMEM((PLANES, LINE, LANES), F32)
+    first = pltpu.VMEM((LINE, PLANES // 4, LANES), F32)
+    second = pltpu.VMEM((PLANES, 2, LANES), F32)
+    third = pltpu.VMEM((PLANES, 2, 2, LANES), F32)
+    fourth = pltpu.VMEM((LINE, 8, LANES), F32)
     points = pltpu.VMEM((3, PT), F32)
     point_index = pltpu.VMEM((1, PT), I32)
     columns = pltpu.VMEM((COLUMN_ROWS, LANES), I32)
@@ -416,7 +442,7 @@
         out_specs=pl.BlockSpec(memory_space=pltpu.VMEM),
         scratch_shapes=[
             points, points, point_index, point_index, columns, columns, columns,
-            by_line, by_line, by_plane, by_plane, by_plane, by_plane, by_line, by_line,
+            first, first, second, second, third, third, fourth, fourth,
             pltpu.VMEM((REPS, 4, PT), F32),
             pltpu.VMEM((STOPS, 4, PT), F32),
             pltpu.VMEM((STOPS, 4, PT), F32),
@@ -426,8 +452,7 @@
             pltpu.VMEM((STOPS, 32, 2 * PT), BF16),
             pltpu.VMEM((REPS, 4, PT), F32),
             pltpu.VMEM((REPS, 4, PT), F32),
-            pltpu.VMEM((CAP, SLOT_ROWS, LANES), I32),
-            pltpu.VMEM((CAP, SLOT_ROWS, LANES), I32),
+            pltpu.VMEM((4, 16, LANES), I32),
             pltpu.VMEM((BLOCKS, PT), BF16),
             dma((7,)), dma((8,)), dma((4,)), dma((REPS,)), dma((STOPS,)), dma((STOPS,)),
             dma((REPS,)),

time: 55.7 us -> 54.4 us (0.977)
  Pallas kernels: 54.1 us -> 52.9 us
    pallas_call x1, Pallas kernels: 54.1 us -> 52.9 us  [shards(): pl.pallas_call(kernel, out_shape=jax.ShapeDtypeStruct((3, PT), F32), in_s...]
where the time goes in v6:
time: 54.4 us; the launch traced here: 54.2 us
  Pallas kernels  52.9 us (97%)
  local copies, waits for them, and re-layouts  1.3 us (2%)
    pallas_call x1, Pallas kernels, shards(): pl.pallas_call(kernel, out_shape=jax.ShapeDtypeStruct((3, PT), F32), in_s...  52.9 us
    unnamed x1, local copies, waits for them, and re-layouts  1.3 us

profile of v6, /device:TPU:1, one launch (start us, length us, event | category | flops | bytes accessed | tf_op | source)
XLA Modules:
  0.0 54.2 jit_solution(18207170470913870595)
XLA Ops:
  0.0 52.9 %shard_map.73 = f32[3,512]{1,0:T(4,128)} custom-call(f32[3,512]{1,0:T(4,128)} %pos_hbm.1, f32[3,512]{1,0:T(4,128)} %flow_hbm.1, s32[1,512]{1,0:T(1,128)} %bitcast.8, s32[1,512]{1,0:T(1,128)} %bitcast.9, s32[10,128]{1,0:T(8,128)} %bitcast.5, s32[10,128]{1,0:T(8,128)} %bitcast.6, s32[10,128]{1,0:T(8,128)} %bitcast.7), custom_call_target="tpu_custom_call" | custom-call | flops 2147483648 | bytes 1048576 | tf_op jit(solution)/shard_map/pallas_call | solution.py:438
  52.9 1.3 %copy.9 = f32[3,512]{1,0:T(4,128)} copy(f32[3,512]{1,0:T(4,128)} %shard_map.73) | data formatting | bytes 12288

commit v7 on v6

--- a/solution.py
+++ b/solution.py
@@ -88,9 +88,9 @@
     pos_hbm, flow_hbm, owner_hbm, slot_hbm, recv_hbm, order_hbm, count_hbm, out_ref,
     pos_ref, flow_ref, owner_ref, slot_ref, recv_ref, order_ref, count_ref,
     out1, in1, turned1, arrived, out2, in2, turned2, returned,
-    targets, src_pos, src_tan, target, features, weights, right, part_out, part_in,
+    targets, src_pos, src_tan, target, features, weights, right, own_sums, part_out, part_in,
     index, member,
-    load_sem, send_sem, phase_sem, rep_sem, pos_sem, tan_sem, part_sem,
+    load_sem, ready, send_sem, phase_sem, rep_sem, pos_sem, tan_sem, part_sem,
 ):
     me = lax.axis_index("blk")
     rep = lax.axis_index("rep")
@@ -102,6 +102,12 @@
 
     def on_plane(k):
         return (plane + k) % PLANES
+
+    def beside_x(k):
+        return (plane + 4 * k) % PLANES
+
+    def beside_y(k):
+        return plane // 4 * 4 + (plane + k) % 4
 
     def on_rep(k):
         return (rep + k) % REPS
@@ -129,12 +135,16 @@
 
     for k in LINE_ORDER:
         greet(plane * LINE + on_line(k), rep)
-    for k in PLANE_ORDER:
-        greet(on_plane(k) * LINE + place, rep)
+    for k in range(1, 4):
+        greet(beside_x(k) * LINE + place, rep)
+        greet(beside_y(k) * LINE + place, rep)
     for k in range(1, REPS):
         greet(me, on_rep(k))
     for stop in STOP_ORDER[1:]:
-        greet(block(stop), rep)
+
+        @pl.when((place + stop < 0) | (place + stop >= LINE))
+        def _():
+            greet(block(stop), rep)
 
     for load in loads[3:]:
         load.start()
@@ -211,9 +221,20 @@
         )
         features[...] = rows.T[:, :FEATURES].astype(BF16)
 
-    def weigh(stop, low, top):
-        def one(k, carry):
-            other = on_rep(k)
+    def weigh(low, top):
+        def one(unit, carry):
+            i = unit // REPS
+            stop = (i % 2) * ((i + 1) // 2) - (1 - i % 2) * (i // 2)
+            other = on_rep(unit % REPS)
+
+            @pl.when((unit % REPS == 0) & (i > 0))
+            def _():
+                await_here(src_pos.at[stop + BACK], pos_sem.at[stop + BACK])
+
+            @pl.when(unit % REPS == 0)
+            def _():
+                describe(stop)
+
             for half in range(PT // 256):
                 low, top = half * 256, half * 256 + 256
                 root = lax.rsqrt(dot(features[...], target[other, :, low:top]))
@@ -227,20 +248,14 @@
 
         lax.fori_loop(low, top, one, 0)
 
-    def weigh_stops(low, top):
-        def one(i, carry):
-            stop = (i % 2) * ((i + 1) // 2) - (1 - i % 2) * (i // 2)
-            await_here(src_pos.at[stop + BACK], pos_sem.at[stop + BACK])
-            describe(stop)
-            weigh(stop, 0, REPS)
-            return carry
-
-        lax.fori_loop(low, top, one, 0)
-
-
-    pl.semaphore_wait(barrier, (LINE - 1) + (PLANES - 1) + (REPS - 1) + (STOPS - 1))
+    across = jnp.where(place < STOPS // 2, STOPS // 2 - place, place - STOPS // 2)
+    pl.semaphore_wait(barrier, (LINE - 1) + 3 + 3 + (REPS - 1) + across)
 
     send_line(out1, in1, 0)
+    for k in range(1, 4):
+        pl.semaphore_signal(
+            ready, inc=1, device_id=(beside_x(k) * LINE + place, rep), device_id_type=MESH
+        )
     for k in range(1, REPS):
         copy_to(targets.at[rep], targets.at[rep], 4, rep_sem.at[rep], me, on_rep(k))
     in1[place] = out1[place]
@@ -271,8 +286,11 @@
         there = jnp.clip(at - order + moved, 0, COLUMN_ROWS * LANES - 1)
         return look_up(inverse, there)
 
+    ahead1, ahead2, behind1, behind2 = (neighbour(k) for k in (1, 2, -1, -2))
+    for i, table in enumerate((ahead1, ahead2, behind1, behind2)):
+        index[i] = table
     aim(rep)
-    describe(0)
+    weigh(0, 1)
     await_here(in1.at[pl.ds(0, LINE - 1)], phase_sem.at[0])
     place_bits, plane_bits = iota((LINE, LANES), 0) >> 1, iota((LINE, LANES), 1) >> 5
     for q in range(PLANES // 4):
@@ -286,19 +304,17 @@
         rows = jnp.where((place_bits >> 1) == (plane_bits >> 1), rows, far_rows)
         for p in range(4):
             turned1[4 * q + p] = rows[2 * p : 2 * p + 2]
+    pl.semaphore_wait(ready, 3)
     send_plane(turned1, arrived, 1)
     arrived[plane] = turned1[plane]
     for stop in STOP_ORDER[1:]:
         copy_to(src_pos.at[BACK], src_pos.at[stop + BACK], 5, pos_sem.at[stop + BACK],
                 block(-stop), rep)
 
-    ahead1, ahead2, behind1, behind2 = (neighbour(k) for k in (1, 2, -1, -2))
-    for i, table in enumerate((ahead1, ahead2, behind1, behind2)):
-        index[i] = table
     for k in range(1, REPS):
         await_here(targets.at[on_rep(k)], rep_sem.at[on_rep(k)])
         aim(on_rep(k))
-    weigh(0, 0, REPS)
+    weigh(1, 4)
 
     await_here(arrived.at[pl.ds(0, PLANES - 1)], phase_sem.at[1])
     rows = arrived[...].reshape(2 * PLANES, LANES)
@@ -330,7 +346,7 @@
 
     send_plane(out2, in2, 2)
     in2[plane] = out2[plane]
-    weigh_stops(1, 3)
+    weigh(4, 14)
     await_here(in2.at[pl.ds(0, PLANES - 1)], phase_sem.at[2])
     left_half = iota((8, LANES), 1) < 64
     for i in range(2):
@@ -341,7 +357,7 @@
             turned2[4 + 2 * i + j] = jnp.where(left_half, pltpu.roll(a, 64, 1), b)
     send_line(turned2, returned, 3)
     returned[place] = turned2[place]
-    weigh_stops(3, 5)
+    weigh(14, 24)
     await_here(returned.at[pl.ds(0, LINE - 1)], phase_sem.at[3])
     rows = returned[...].reshape(64, LANES)
     back = jnp.concatenate([rows, pltpu.roll(rows, 64, 1)], axis=0).T[:64]
@@ -356,7 +372,7 @@
     for stop in STOP_ORDER[1:]:
         copy_to(src_tan.at[BACK], src_tan.at[stop + BACK], 6, tan_sem.at[stop + BACK],
                 block(-stop), rep)
-    weigh_stops(5, STOPS)
+    weigh(24, SOURCES)
 
     def prepare(stop):
         p, t = rows_of(src_pos[stop], 0, 3), rows_of(src_tan[stop], 0, 3)
@@ -366,6 +382,8 @@
         right[stop, :, PT:] = rows
 
     prepare(BACK)
+    for k in range(REPS):
+        own_sums[k] = dot(right[BACK], weights[k, BACK])
     for stop in STOP_ORDER[1:]:
         await_here(src_tan.at[stop + BACK], tan_sem.at[stop + BACK])
         prepare(stop + BACK)
@@ -373,12 +391,9 @@
     def gather_sums(k):
         other = on_rep(k)
 
-        def some(i, sums):
-            for j in range(4):
-                sums = sums + dot(right[4 * i + j], weights[other, 4 * i + j])
-            return sums
-
-        parts = lax.fori_loop(0, STOPS // 4, some, jnp.zeros((32, PT), F32))
+        parts = own_sums[other]
+        for stop in STOP_ORDER[:0:-1]:
+            parts = parts + dot(right[stop + BACK], weights[other, stop + BACK])
         parts = parts[0:8] + parts[8:16] + parts[16:24]
         far = cross(rows_of(parts, 0, 3), rows_of(targets[other], 0, 3))
         part_out[k % REPS] = jnp.concatenate(
@@ -450,28 +465,34 @@
             pltpu.VMEM((PT, FEATURES), BF16),
             pltpu.VMEM((REPS, STOPS, 2 * PT, PT), BF16),
             pltpu.VMEM((STOPS, 32, 2 * PT), BF16),
+            pltpu.VMEM((REPS, 32, PT), F32),
             pltpu.VMEM((REPS, 4, PT), F32),
             pltpu.VMEM((REPS, 4, PT), F32),
             pltpu.VMEM((4, 16, LANES), I32),
             pltpu.VMEM((BLOCKS, PT), BF16),
-            dma((7,)), dma((8,)), dma((4,)), dma((REPS,)), dma((STOPS,)), dma((STOPS,)),
+            dma((7,)), pltpu.SemaphoreType.REGULAR, dma((8,)), dma((4,)), dma((REPS,)), dma((STOPS,)), dma((STOPS,)),
             dma((REPS,)),
         ],
         compiler_params=pltpu.CompilerParams(
-            collective_id=0, has_side_effects=True, vmem_limit_bytes=60 * 1024 * 1024
+            collective_id=0, has_side_effects=True, vmem_limit_bytes=48 * 1024 * 1024
         ),
         cost_estimate=pl.CostEstimate(
             flops=2 * PT * SOURCES * PT * 128, bytes_accessed=1 << 20,
             transcendentals=PT * SOURCES * PT,
         ),
     )(
-        positions,
-        normal_flow,
-        send_owner.reshape(1, PT),
-        send_slot.reshape(1, PT),
-        recv_index.reshape(CAP, BLOCKS),
-        loop_pos.reshape(COLUMN_ROWS, LANES),
-        loop_len.reshape(COLUMN_ROWS, LANES),
+        *(
+            pltpu.with_memory_space_constraint(operand, pltpu.HBM)
+            for operand in (
+                positions,
+                normal_flow,
+                send_owner.reshape(1, PT),
+                send_slot.reshape(1, PT),
+                recv_index.reshape(CAP, BLOCKS),
+                loop_pos.reshape(COLUMN_ROWS, LANES),
+                loop_len.reshape(COLUMN_ROWS, LANES),
+            )
+        )
     )
 
 

time: 54.4 us -> 53.8 us (0.989)
  local copies, waits for them, and re-layouts: 1.3 us -> 0.6 us
    unnamed x1, local copies, waits for them, and re-layouts: 1.3 us -> 0.6 us
where the time goes in v7:
time: 53.8 us; the launch traced here: 53.6 us
  Pallas kernels  53 us (99%)
  local copies, waits for them, and re-layouts  0.6 us (1%)
    pallas_call x1, Pallas kernels, shards(): pl.pallas_call(kernel, out_shape=jax.ShapeDtypeStruct((3, PT), F32), in_s...  53 us

profile of v7, /device:TPU:1, one launch (start us, length us, event | category | flops | bytes accessed | tf_op | source)
XLA Modules:
  0.0 53.6 jit_solution(12279095216578733276)
XLA Ops:
  0.0 53.0 %shard_map.73 = f32[3,512]{1,0:T(4,128)S(1)} custom-call(f32[3,512]{1,0:T(4,128)} %pos_hbm.1, f32[3,512]{1,0:T(4,128)} %flow_hbm.1, s32[1,512]{1,0:T(1,128)} %bitcast.8, s32[1,512]{1,0:T(1,128)} %bitcast.9, s32[10,128]{1,0:T(8,128)} %bitcast.5, s32[10,128]{1,0:T(8,128)} %bitcast.6, s32[10,128]{1,0:T(8,128)} %bitcast.7), custom_call_target="tpu_custom_call" | custom-call | flops 2147483648 | bytes 1048576 | tf_op jit(solution)/shard_map/pallas_call | solution.py:453
  53.0 0.6 %copy.9 = f32[3,512]{1,0:T(4,128)} copy(f32[3,512]{1,0:T(4,128)S(1)} %shard_map.73) | data formatting | bytes 12288

commit v8 on v7

--- a/solution.py
+++ b/solution.py
@@ -88,7 +88,7 @@
     pos_hbm, flow_hbm, owner_hbm, slot_hbm, recv_hbm, order_hbm, count_hbm, out_ref,
     pos_ref, flow_ref, owner_ref, slot_ref, recv_ref, order_ref, count_ref,
     out1, in1, turned1, arrived, out2, in2, turned2, returned,
-    targets, src_pos, src_tan, target, features, weights, right, own_sums, part_out, part_in,
+    targets, src_pos, src_tan, target, features, weights, weights_a, weights_b, right, own_sums, part_out, part_in,
     index, member,
     load_sem, ready, send_sem, phase_sem, rep_sem, pos_sem, tan_sem, part_sem,
 ):
@@ -221,29 +221,27 @@
         )
         features[...] = rows.T[:, :FEATURES].astype(BF16)
 
-    def weigh(low, top):
-        def one(unit, carry):
-            i = unit // REPS
-            stop = (i % 2) * ((i + 1) // 2) - (1 - i % 2) * (i // 2)
-            other = on_rep(unit % REPS)
-
-            @pl.when((unit % REPS == 0) & (i > 0))
-            def _():
-                await_here(src_pos.at[stop + BACK], pos_sem.at[stop + BACK])
-
-            @pl.when(unit % REPS == 0)
-            def _():
-                describe(stop)
-
+    def weigh(stop, held, beside=None):
+        describe(stop)
+        for other in range(REPS):
             for half in range(PT // 256):
                 low, top = half * 256, half * 256 + 256
                 root = lax.rsqrt(dot(features[...], target[other, :, low:top]))
                 weight = root * root * root
                 high = weight.astype(BF16)
-                weights[other, stop + BACK, :PT, low:top] = high
-                weights[other, stop + BACK, PT:, low:top] = (
-                    weight - high.astype(F32)
-                ).astype(BF16)
+                held[other, :PT, low:top] = high
+                held[other, PT:, low:top] = (weight - high.astype(F32)).astype(BF16)
+            if beside is not None:
+                beside(other)
+
+    def await_pos(stop):
+        await_here(src_pos.at[stop + BACK], pos_sem.at[stop + BACK])
+
+    def weigh_stops(low, top):
+        def one(i, carry):
+            stop = (i % 2) * ((i + 1) // 2) - (1 - i % 2) * (i // 2)
+            await_pos(stop)
+            weigh(stop, weights.at[stop + BACK - 1])
             return carry
 
         lax.fori_loop(low, top, one, 0)
@@ -290,7 +288,6 @@
     for i, table in enumerate((ahead1, ahead2, behind1, behind2)):
         index[i] = table
     aim(rep)
-    weigh(0, 1)
     await_here(in1.at[pl.ds(0, LINE - 1)], phase_sem.at[0])
     place_bits, plane_bits = iota((LINE, LANES), 0) >> 1, iota((LINE, LANES), 1) >> 5
     for q in range(PLANES // 4):
@@ -314,7 +311,7 @@
     for k in range(1, REPS):
         await_here(targets.at[on_rep(k)], rep_sem.at[on_rep(k)])
         aim(on_rep(k))
-    weigh(1, 4)
+    weigh(0, weights.at[BACK - 1])
 
     await_here(arrived.at[pl.ds(0, PLANES - 1)], phase_sem.at[1])
     rows = arrived[...].reshape(2 * PLANES, LANES)
@@ -346,7 +343,7 @@
 
     send_plane(out2, in2, 2)
     in2[plane] = out2[plane]
-    weigh(4, 14)
+    weigh_stops(1, 3)
     await_here(in2.at[pl.ds(0, PLANES - 1)], phase_sem.at[2])
     left_half = iota((8, LANES), 1) < 64
     for i in range(2):
@@ -357,7 +354,7 @@
             turned2[4 + 2 * i + j] = jnp.where(left_half, pltpu.roll(a, 64, 1), b)
     send_line(turned2, returned, 3)
     returned[place] = turned2[place]
-    weigh(14, 24)
+    weigh_stops(3, 5)
     await_here(returned.at[pl.ds(0, LINE - 1)], phase_sem.at[3])
     rows = returned[...].reshape(64, LANES)
     back = jnp.concatenate([rows, pltpu.roll(rows, 64, 1)], axis=0).T[:64]
@@ -372,7 +369,6 @@
     for stop in STOP_ORDER[1:]:
         copy_to(src_tan.at[BACK], src_tan.at[stop + BACK], 6, tan_sem.at[stop + BACK],
                 block(-stop), rep)
-    weigh(24, SOURCES)
 
     def prepare(stop):
         p, t = rows_of(src_pos[stop], 0, 3), rows_of(src_tan[stop], 0, 3)
@@ -381,19 +377,40 @@
         right[stop, :, :PT] = rows
         right[stop, :, PT:] = rows
 
+    def held_of(stop):
+        return weights_a if stop == -3 else weights_b if stop == 4 else weights.at[stop + BACK - 1]
+
+    def add_sums(stops):
+        def one(other):
+            sums = [dot(right[stop + BACK], held_of(stop)[other]) for stop in stops]
+            sums = functools.reduce(jnp.add, sums)
+            own_sums[other] = sums if 0 in stops else own_sums[other] + sums
+
+        return one
+
+    def receive(stops):
+        for stop in stops:
+            await_here(src_tan.at[stop + BACK], tan_sem.at[stop + BACK])
+            prepare(stop + BACK)
+
     prepare(BACK)
-    for k in range(REPS):
-        own_sums[k] = dot(right[BACK], weights[k, BACK])
-    for stop in STOP_ORDER[1:]:
-        await_here(src_tan.at[stop + BACK], tan_sem.at[stop + BACK])
-        prepare(stop + BACK)
+    await_pos(3)
+    weigh(3, weights.at[3 + BACK - 1], add_sums([0]))
+    await_pos(-3)
+    receive([1, -1, 2])
+    weigh(-3, weights_a, add_sums([1, -1, 2]))
+    await_pos(4)
+    receive([-2, 3])
+    weigh(4, weights_b, add_sums([-2, 3]))
+    receive([-3, 4])
 
     def gather_sums(k):
         other = on_rep(k)
-
-        parts = own_sums[other]
-        for stop in STOP_ORDER[:0:-1]:
-            parts = parts + dot(right[stop + BACK], weights[other, stop + BACK])
+        parts = (
+            own_sums[other]
+            + dot(right[BACK - 3], weights_a[other])
+            + dot(right[BACK + 4], weights_b[other])
+        )
         parts = parts[0:8] + parts[8:16] + parts[16:24]
         far = cross(rows_of(parts, 0, 3), rows_of(targets[other], 0, 3))
         part_out[k % REPS] = jnp.concatenate(
@@ -463,7 +480,9 @@
             pltpu.VMEM((STOPS, 4, PT), F32),
             pltpu.VMEM((REPS, FEATURES, PT), BF16),
             pltpu.VMEM((PT, FEATURES), BF16),
-            pltpu.VMEM((REPS, STOPS, 2 * PT, PT), BF16),
+            pltpu.VMEM((STOPS - 2, REPS, 2 * PT, PT), BF16),
+            pltpu.VMEM((REPS, 2 * PT, PT), BF16),
+            pltpu.VMEM((REPS, 2 * PT, PT), BF16),
             pltpu.VMEM((STOPS, 32, 2 * PT), BF16),
             pltpu.VMEM((REPS, 32, PT), F32),
             pltpu.VMEM((REPS, 4, PT), F32),

time: 53.8 us -> 53.9 us (level)
  no operation moved by 1% of the time
where the time goes in v8:
time: 53.9 us; the launch traced here: 53.8 us
  Pallas kernels  53.2 us (99%)
  local copies, waits for them, and re-layouts  0.6 us (1%)
    pallas_call x1, Pallas kernels, shards(): pl.pallas_call(kernel, out_shape=jax.ShapeDtypeStruct((3, PT), F32), in_s...  53.2 us

profile of v8, /device:TPU:1, one launch (start us, length us, event | category | flops | bytes accessed | tf_op | source)
XLA Modules:
  0.0 53.8 jit_solution(10028559382349757193)
XLA Ops:
  0.0 53.2 %shard_map.73 = f32[3,512]{1,0:T(4,128)S(1)} custom-call(f32[3,512]{1,0:T(4,128)} %pos_hbm.1, f32[3,512]{1,0:T(4,128)} %flow_hbm.1, s32[1,512]{1,0:T(1,128)} %bitcast.8, s32[1,512]{1,0:T(1,128)} %bitcast.9, s32[10,128]{1,0:T(8,128)} %bitcast.5, s32[10,128]{1,0:T(8,128)} %bitcast.6, s32[10,128]{1,0:T(8,128)} %bitcast.7), custom_call_target="tpu_custom_call" | custom-call | flops 2147483648 | bytes 1048576 | tf_op jit(solution)/shard_map/pallas_call | solution.py:470
  53.2 0.6 %copy.9 = f32[3,512]{1,0:T(4,128)} copy(f32[3,512]{1,0:T(4,128)S(1)} %shard_map.73) | data formatting | bytes 12288

commit v9 on v7

--- a/solution.py
+++ b/solution.py
@@ -378,41 +378,52 @@
         p, t = rows_of(src_pos[stop], 0, 3), rows_of(src_tan[stop], 0, 3)
         h, m, l = split(jnp.concatenate(t + cross(t, p) + [jnp.zeros((2, PT), F32)], axis=0))
         rows = jnp.concatenate([h, m, l, jnp.zeros((8, PT), F32)], axis=0).astype(BF16)
-        right[stop, :, :PT] = rows
-        right[stop, :, PT:] = rows
+        rows = jnp.concatenate([rows, rows], axis=1)
+        right[stop] = rows
+        return rows
 
     prepare(BACK)
     for k in range(REPS):
         own_sums[k] = dot(right[BACK], weights[k, BACK])
     for stop in STOP_ORDER[1:]:
         await_here(src_tan.at[stop + BACK], tan_sem.at[stop + BACK])
-        prepare(stop + BACK)
-
-    def gather_sums(k):
-        other = on_rep(k)
-
+
+    def finish_sums(i, other, parts):
+        parts = parts[0:8] + parts[8:16] + parts[16:24]
+        far = cross(rows_of(parts, 0, 3), rows_of(targets[other], 0, 3))
+        part_out[i] = jnp.concatenate(
+            [far[c] - parts[3 + c : 4 + c] for c in range(3)] + [jnp.zeros((1, PT), F32)], axis=0
+        )
+
+    def send_sums(i, other):
+        copy_to(part_out.at[i], part_in.at[i], 7, part_sem.at[i], me, other)
+
+    other = (rep + 2) % REPS
+    parts = own_sums[other]
+    for stop in STOP_ORDER[:0:-1]:
+        parts = parts + dot(prepare(stop + BACK), weights[other, stop + BACK])
+    finish_sums(0, other, parts)
+    send_sums(0, other)
+
+    def sums_of(i, carry):
+        other = jnp.where(
+            i == 1, REPS - 1 - rep, jnp.where(i == 2, rep + 1 - 2 * (rep % 2), rep)
+        )
         parts = own_sums[other]
         for stop in STOP_ORDER[:0:-1]:
             parts = parts + dot(right[stop + BACK], weights[other, stop + BACK])
-        parts = parts[0:8] + parts[8:16] + parts[16:24]
-        far = cross(rows_of(parts, 0, 3), rows_of(targets[other], 0, 3))
-        part_out[k % REPS] = jnp.concatenate(
-            [far[c] - parts[3 + c : 4 + c] for c in range(3)] + [jnp.zeros((1, PT), F32)], axis=0
-        )
-
-    def sums_of(k, carry):
-        gather_sums(k)
-
-        @pl.when(k < REPS)
+        finish_sums(i, other, parts)
+
+        @pl.when(i < REPS - 1)
         def _():
-            copy_to(part_out.at[k], part_in.at[k], 7, part_sem.at[k], me, on_rep(k))
+            send_sums(i, other)
 
         return carry
 
-    lax.fori_loop(1, REPS + 1, sums_of, 0)
-    for k in range(1, REPS):
-        await_here(part_in.at[k], part_sem.at[k])
-    others = part_out[0] + part_in[1] + part_in[2] + part_in[3]
+    lax.fori_loop(1, REPS, sums_of, 0)
+    for i in range(REPS - 1):
+        await_here(part_in.at[i], part_sem.at[i])
+    others = part_out[REPS - 1] + part_in[0] + part_in[1] + part_in[2]
     far = [others[c : c + 1] for c in range(3)]
 
     tangent, curvature = derived[0:3], derived[3:6]
@@ -438,7 +449,7 @@
     await_sent(targets.at[pl.ds(0, REPS - 1)], 4)
     await_sent(src_pos.at[pl.ds(0, STOPS - 1)], 5)
     await_sent(src_tan.at[pl.ds(0, STOPS - 1)], 6)
-    await_sent(part_out.at[pl.ds(1, REPS - 1)], 7)
+    await_sent(part_out.at[pl.ds(0, REPS - 1)], 7)
 
 
 def shards(positions, normal_flow, send_owner, send_slot, recv_index, loop_pos, loop_len):

time: 53.8 us -> 52.2 us (0.970)
  Pallas kernels: 53 us -> 51.5 us
    pallas_call x1, Pallas kernels: 53 us -> 51.5 us  [shards(): pl.pallas_call(kernel, out_shape=jax.ShapeDtypeStruct((3, PT), F32), in_s...]
where the time goes in v9:
time: 52.2 us; the launch traced here: 52.1 us
  Pallas kernels  51.5 us (99%)
  local copies, waits for them, and re-layouts  0.6 us (1%)
    pallas_call x1, Pallas kernels, shards(): pl.pallas_call(kernel, out_shape=jax.ShapeDtypeStruct((3, PT), F32), in_s...  51.5 us

profile of v9, /device:TPU:1, one launch (start us, length us, event | category | flops | bytes accessed | tf_op | source)
XLA Modules:
  0.0 52.1 jit_solution(17421161109896113166)
XLA Ops:
  0.0 51.5 %shard_map.73 = f32[3,512]{1,0:T(4,128)S(1)} custom-call(f32[3,512]{1,0:T(4,128)} %pos_hbm.1, f32[3,512]{1,0:T(4,128)} %flow_hbm.1, s32[1,512]{1,0:T(1,128)} %bitcast.8, s32[1,512]{1,0:T(1,128)} %bitcast.9, s32[10,128]{1,0:T(8,128)} %bitcast.5, s32[10,128]{1,0:T(8,128)} %bitcast.6, s32[10,128]{1,0:T(8,128)} %bitcast.7), custom_call_target="tpu_custom_call" | custom-call | flops 2147483648 | bytes 1048576 | tf_op jit(solution)/shard_map/pallas_call | solution.py:464
  51.5 0.6 %copy.9 = f32[3,512]{1,0:T(4,128)} copy(f32[3,512]{1,0:T(4,128)S(1)} %shard_map.73) | data formatting | bytes 12288

commit v10 on v9

--- a/solution.py
+++ b/solution.py
@@ -35,6 +35,8 @@
 F32 = jnp.float32
 BF16 = jnp.bfloat16
 I32 = jnp.int32
+F8 = jnp.float8_e4m3fn
+LOW_SCALE = 8192.0
 
 NT = (((1,), (1,)), ((), ()))
 NN = (((1,), (0,)), ((), ()))
@@ -88,7 +90,7 @@
     pos_hbm, flow_hbm, owner_hbm, slot_hbm, recv_hbm, order_hbm, count_hbm, out_ref,
     pos_ref, flow_ref, owner_ref, slot_ref, recv_ref, order_ref, count_ref,
     out1, in1, turned1, arrived, out2, in2, turned2, returned,
-    targets, src_pos, src_tan, target, features, weights, right, own_sums, part_out, part_in,
+    targets, src_pos, src_tan, target, features, weights, weights_low, right, right_low, own_sums, part_out, part_in,
     index, member,
     load_sem, ready, send_sem, phase_sem, rep_sem, pos_sem, tan_sem, part_sem,
 ):
@@ -179,8 +181,9 @@
         ).start()
 
     def send_line(src, dst, phase):
-        for k in LINE_ORDER:
-            there = on_line(k)
+        for k in range(1, LINE) if phase == 0 else LINE_ORDER:
+            late = jnp.where(LINE - k > place, LINE - k, LINE - 1 - k)
+            there = late if phase == 0 else on_line(k)
             copy_to(src.at[there], dst.at[place], phase, phase_sem.at[phase],
                     plane * LINE + there, rep)
 
@@ -240,10 +243,9 @@
                 root = lax.rsqrt(dot(features[...], target[other, :, low:top]))
                 weight = root * root * root
                 high = weight.astype(BF16)
-                weights[other, stop + BACK, :PT, low:top] = high
-                weights[other, stop + BACK, PT:, low:top] = (
-                    weight - high.astype(F32)
-                ).astype(BF16)
+                weights[other, stop + BACK, :, low:top] = high
+                rest = (weight - high.astype(F32)) * LOW_SCALE
+                weights_low[other, stop + BACK, :, low:top] = rest.astype(F8)
             return carry
 
         lax.fori_loop(low, top, one, 0)
@@ -376,15 +378,28 @@
 
     def prepare(stop):
         p, t = rows_of(src_pos[stop], 0, 3), rows_of(src_tan[stop], 0, 3)
-        h, m, l = split(jnp.concatenate(t + cross(t, p) + [jnp.zeros((2, PT), F32)], axis=0))
-        rows = jnp.concatenate([h, m, l, jnp.zeros((8, PT), F32)], axis=0).astype(BF16)
-        rows = jnp.concatenate([rows, rows], axis=1)
-        right[stop] = rows
-        return rows
+        rows = jnp.concatenate(t + cross(t, p) + [jnp.zeros((2, PT), F32)], axis=0)
+        h, m, l = split(rows)
+        right[stop] = jnp.concatenate([h, m, l, jnp.zeros((8, PT), F32)], axis=0).astype(BF16)
+        high = rows.astype(F8).astype(F32)
+        right_low[stop] = jnp.concatenate(
+            [high, rows - high, jnp.zeros((16, PT), F32)], axis=0
+        ).astype(F8)
+
+    def product(other, stop):
+        high = dot(right[stop + BACK], weights[other, stop + BACK])
+        low = dot(right_low[stop + BACK], weights_low[other, stop + BACK])
+        return high + low * (1.0 / LOW_SCALE)
 
     prepare(BACK)
     for k in range(REPS):
-        own_sums[k] = dot(right[BACK], weights[k, BACK])
+        own_sums[k] = product(k, 0)
+    await_sent(out1.at[pl.ds(0, LINE - 1)], 0)
+    await_sent(turned1.at[pl.ds(0, PLANES - 1)], 1)
+    await_sent(out2.at[pl.ds(0, PLANES - 1)], 2)
+    await_sent(turned2.at[pl.ds(0, LINE - 1)], 3)
+    await_sent(targets.at[pl.ds(0, REPS - 1)], 4)
+    await_sent(src_pos.at[pl.ds(0, STOPS - 1)], 5)
     for stop in STOP_ORDER[1:]:
         await_here(src_tan.at[stop + BACK], tan_sem.at[stop + BACK])
 
@@ -401,7 +416,8 @@
     other = (rep + 2) % REPS
     parts = own_sums[other]
     for stop in STOP_ORDER[:0:-1]:
-        parts = parts + dot(prepare(stop + BACK), weights[other, stop + BACK])
+        prepare(stop + BACK)
+        parts = parts + product(other, stop)
     finish_sums(0, other, parts)
     send_sums(0, other)
 
@@ -411,7 +427,7 @@
         )
         parts = own_sums[other]
         for stop in STOP_ORDER[:0:-1]:
-            parts = parts + dot(right[stop + BACK], weights[other, stop + BACK])
+            parts = parts + product(other, stop)
         finish_sums(i, other, parts)
 
         @pl.when(i < REPS - 1)
@@ -442,12 +458,6 @@
             superfluid[c] + FRICTION_ALPHA * once[c] - FRICTION_PRIME * twice[c]
         )
 
-    await_sent(out1.at[pl.ds(0, LINE - 1)], 0)
-    await_sent(turned1.at[pl.ds(0, PLANES - 1)], 1)
-    await_sent(out2.at[pl.ds(0, PLANES - 1)], 2)
-    await_sent(turned2.at[pl.ds(0, LINE - 1)], 3)
-    await_sent(targets.at[pl.ds(0, REPS - 1)], 4)
-    await_sent(src_pos.at[pl.ds(0, STOPS - 1)], 5)
     await_sent(src_tan.at[pl.ds(0, STOPS - 1)], 6)
     await_sent(part_out.at[pl.ds(0, REPS - 1)], 7)
 
@@ -474,8 +484,10 @@
             pltpu.VMEM((STOPS, 4, PT), F32),
             pltpu.VMEM((REPS, FEATURES, PT), BF16),
             pltpu.VMEM((PT, FEATURES), BF16),
-            pltpu.VMEM((REPS, STOPS, 2 * PT, PT), BF16),
-            pltpu.VMEM((STOPS, 32, 2 * PT), BF16),
+            pltpu.VMEM((REPS, STOPS, PT, PT), BF16),
+            pltpu.VMEM((REPS, STOPS, PT, PT), F8),
+            pltpu.VMEM((STOPS, 32, PT), BF16),
+            pltpu.VMEM((STOPS, 32, PT), F8),
             pltpu.VMEM((REPS, 32, PT), F32),
             pltpu.VMEM((REPS, 4, PT), F32),
             pltpu.VMEM((REPS, 4, PT), F32),
@@ -485,7 +497,7 @@
             dma((REPS,)),
         ],
         compiler_params=pltpu.CompilerParams(
-            collective_id=0, has_side_effects=True, vmem_limit_bytes=48 * 1024 * 1024
+            collective_id=0, has_side_effects=True, vmem_limit_bytes=40 * 1024 * 1024
         ),
         cost_estimate=pl.CostEstimate(
             flops=2 * PT * SOURCES * PT * 128, bytes_accessed=1 << 20,

time: 52.2 us -> 52.2 us (level)
  no operation moved by 1% of the time
where the time goes in v10:
time: 52.2 us; the launch traced here: 52.1 us
  Pallas kernels  51.5 us (99%)
  local copies, waits for them, and re-layouts  0.6 us (1%)
    pallas_call x1, Pallas kernels, shards(): pl.pallas_call(kernel, out_shape=jax.ShapeDtypeStruct((3, PT), F32), in_s...  51.5 us

profile of v10, /device:TPU:1, one launch (start us, length us, event | category | flops | bytes accessed | tf_op | source)
XLA Modules:
  0.0 52.1 jit_solution(13435446542972276221)
XLA Ops:
  0.0 51.5 %shard_map.73 = f32[3,512]{1,0:T(4,128)S(1)} custom-call(f32[3,512]{1,0:T(4,128)} %pos_hbm.1, f32[3,512]{1,0:T(4,128)} %flow_hbm.1, s32[1,512]{1,0:T(1,128)} %bitcast.8, s32[1,512]{1,0:T(1,128)} %bitcast.9, s32[10,128]{1,0:T(8,128)} %bitcast.5, s32[10,128]{1,0:T(8,128)} %bitcast.6, s32[10,128]{1,0:T(8,128)} %bitcast.7), custom_call_target="tpu_custom_call" | custom-call | flops 2147483648 | bytes 1048576 | tf_op jit(solution)/shard_map/pallas_call | solution.py:474
  51.5 0.6 %copy.9 = f32[3,512]{1,0:T(4,128)} copy(f32[3,512]{1,0:T(4,128)S(1)} %shard_map.73) | data formatting | bytes 12288

commit v11 on v9

--- a/solution.py
+++ b/solution.py
@@ -125,16 +125,16 @@
             ]
         )
     ]
+
+    barrier = pltpu.get_barrier_semaphore()
+
+    def greet(blk, other):
+        pl.semaphore_signal(barrier, inc=1, device_id=(blk, other), device_id_type=MESH)
+
+    for k in LINE_ORDER:
+        greet(plane * LINE + on_line(k), rep)
     for load in loads[:3]:
         load.start()
-
-    barrier = pltpu.get_barrier_semaphore()
-
-    def greet(blk, other):
-        pl.semaphore_signal(barrier, inc=1, device_id=(blk, other), device_id_type=MESH)
-
-    for k in LINE_ORDER:
-        greet(plane * LINE + on_line(k), rep)
     for k in range(1, 4):
         greet(beside_x(k) * LINE + place, rep)
         greet(beside_y(k) * LINE + place, rep)
@@ -179,8 +179,9 @@
         ).start()
 
     def send_line(src, dst, phase):
-        for k in LINE_ORDER:
-            there = on_line(k)
+        for k in range(1, LINE) if phase == 0 else LINE_ORDER:
+            late = jnp.where(LINE - k > place, LINE - k, LINE - 1 - k)
+            there = late if phase == 0 else on_line(k)
             copy_to(src.at[there], dst.at[place], phase, phase_sem.at[phase],
                     plane * LINE + there, rep)
 
@@ -346,7 +347,7 @@
 
     send_plane(out2, in2, 2)
     in2[plane] = out2[plane]
-    weigh(4, 14)
+    weigh(4, 16)
     await_here(in2.at[pl.ds(0, PLANES - 1)], phase_sem.at[2])
     left_half = iota((8, LANES), 1) < 64
     for i in range(2):
@@ -357,7 +358,7 @@
             turned2[4 + 2 * i + j] = jnp.where(left_half, pltpu.roll(a, 64, 1), b)
     send_line(turned2, returned, 3)
     returned[place] = turned2[place]
-    weigh(14, 24)
+    weigh(16, 28)
     await_here(returned.at[pl.ds(0, LINE - 1)], phase_sem.at[3])
     rows = returned[...].reshape(64, LANES)
     back = jnp.concatenate([rows, pltpu.roll(rows, 64, 1)], axis=0).T[:64]
@@ -372,7 +373,7 @@
     for stop in STOP_ORDER[1:]:
         copy_to(src_tan.at[BACK], src_tan.at[stop + BACK], 6, tan_sem.at[stop + BACK],
                 block(-stop), rep)
-    weigh(24, SOURCES)
+    weigh(28, SOURCES)
 
     def prepare(stop):
         p, t = rows_of(src_pos[stop], 0, 3), rows_of(src_tan[stop], 0, 3)
@@ -385,6 +386,12 @@
     prepare(BACK)
     for k in range(REPS):
         own_sums[k] = dot(right[BACK], weights[k, BACK])
+    await_sent(out1.at[pl.ds(0, LINE - 1)], 0)
+    await_sent(turned1.at[pl.ds(0, PLANES - 1)], 1)
+    await_sent(out2.at[pl.ds(0, PLANES - 1)], 2)
+    await_sent(turned2.at[pl.ds(0, LINE - 1)], 3)
+    await_sent(targets.at[pl.ds(0, REPS - 1)], 4)
+    await_sent(src_pos.at[pl.ds(0, STOPS - 1)], 5)
     for stop in STOP_ORDER[1:]:
         await_here(src_tan.at[stop + BACK], tan_sem.at[stop + BACK])
 
@@ -442,12 +449,6 @@
             superfluid[c] + FRICTION_ALPHA * once[c] - FRICTION_PRIME * twice[c]
         )
 
-    await_sent(out1.at[pl.ds(0, LINE - 1)], 0)
-    await_sent(turned1.at[pl.ds(0, PLANES - 1)], 1)
-    await_sent(out2.at[pl.ds(0, PLANES - 1)], 2)
-    await_sent(turned2.at[pl.ds(0, LINE - 1)], 3)
-    await_sent(targets.at[pl.ds(0, REPS - 1)], 4)
-    await_sent(src_pos.at[pl.ds(0, STOPS - 1)], 5)
     await_sent(src_tan.at[pl.ds(0, STOPS - 1)], 6)
     await_sent(part_out.at[pl.ds(0, REPS - 1)], 7)
 

time: 52.2 us -> 54.1 us (1.036)
  Pallas kernels: 51.5 us -> 53.4 us
    pallas_call x1, Pallas kernels: 51.5 us -> 53.4 us  [shards(): pl.pallas_call(kernel, out_shape=jax.ShapeDtypeStruct((3, PT), F32), in_s...]
where the time goes in v11:
time: 54.1 us; the launch traced here: 54 us
  Pallas kernels  53.4 us (99%)
  local copies, waits for them, and re-layouts  0.6 us (1%)
    pallas_call x1, Pallas kernels, shards(): pl.pallas_call(kernel, out_shape=jax.ShapeDtypeStruct((3, PT), F32), in_s...  53.4 us

profile of v11, /device:TPU:1, one launch (start us, length us, event | category | flops | bytes accessed | tf_op | source)
XLA Modules:
  0.0 54.0 jit_solution(2302960378402547689)
XLA Ops:
  0.0 53.4 %shard_map.73 = f32[3,512]{1,0:T(4,128)S(1)} custom-call(f32[3,512]{1,0:T(4,128)} %pos_hbm.1, f32[3,512]{1,0:T(4,128)} %flow_hbm.1, s32[1,512]{1,0:T(1,128)} %bitcast.8, s32[1,512]{1,0:T(1,128)} %bitcast.9, s32[10,128]{1,0:T(8,128)} %bitcast.5, s32[10,128]{1,0:T(8,128)} %bitcast.6, s32[10,128]{1,0:T(8,128)} %bitcast.7), custom_call_target="tpu_custom_call" | custom-call | flops 2147483648 | bytes 1048576 | tf_op jit(solution)/shard_map/pallas_call | solution.py:465
  53.4 0.6 %copy.9 = f32[3,512]{1,0:T(4,128)} copy(f32[3,512]{1,0:T(4,128)S(1)} %shard_map.73) | data formatting | bytes 12288

commit v12 on v9

--- a/solution.py
+++ b/solution.py
@@ -346,7 +346,7 @@
 
     send_plane(out2, in2, 2)
     in2[plane] = out2[plane]
-    weigh(4, 14)
+    weigh(4, 10)
     await_here(in2.at[pl.ds(0, PLANES - 1)], phase_sem.at[2])
     left_half = iota((8, LANES), 1) < 64
     for i in range(2):
@@ -357,7 +357,7 @@
             turned2[4 + 2 * i + j] = jnp.where(left_half, pltpu.roll(a, 64, 1), b)
     send_line(turned2, returned, 3)
     returned[place] = turned2[place]
-    weigh(14, 24)
+    weigh(10, 16)
     await_here(returned.at[pl.ds(0, LINE - 1)], phase_sem.at[3])
     rows = returned[...].reshape(64, LANES)
     back = jnp.concatenate([rows, pltpu.roll(rows, 64, 1)], axis=0).T[:64]
@@ -372,7 +372,7 @@
     for stop in STOP_ORDER[1:]:
         copy_to(src_tan.at[BACK], src_tan.at[stop + BACK], 6, tan_sem.at[stop + BACK],
                 block(-stop), rep)
-    weigh(24, SOURCES)
+    weigh(16, SOURCES)
 
     def prepare(stop):
         p, t = rows_of(src_pos[stop], 0, 3), rows_of(src_tan[stop], 0, 3)

time: 52.2 us -> 53.7 us (1.029)
  Pallas kernels: 51.5 us -> 52.9 us
    pallas_call x1, Pallas kernels: 51.5 us -> 52.9 us  [shards(): pl.pallas_call(kernel, out_shape=jax.ShapeDtypeStruct((3, PT), F32), in_s...]
where the time goes in v12:
time: 53.7 us; the launch traced here: 53.5 us
  Pallas kernels  52.9 us (99%)
  local copies, waits for them, and re-layouts  0.6 us (1%)
    pallas_call x1, Pallas kernels, shards(): pl.pallas_call(kernel, out_shape=jax.ShapeDtypeStruct((3, PT), F32), in_s...  52.9 us

profile of v12, /device:TPU:1, one launch (start us, length us, event | category | flops | bytes accessed | tf_op | source)
XLA Modules:
  0.0 53.5 jit_solution(8766887243928981591)
XLA Ops:
  0.0 52.9 %shard_map.73 = f32[3,512]{1,0:T(4,128)S(1)} custom-call(f32[3,512]{1,0:T(4,128)} %pos_hbm.1, f32[3,512]{1,0:T(4,128)} %flow_hbm.1, s32[1,512]{1,0:T(1,128)} %bitcast.8, s32[1,512]{1,0:T(1,128)} %bitcast.9, s32[10,128]{1,0:T(8,128)} %bitcast.5, s32[10,128]{1,0:T(8,128)} %bitcast.6, s32[10,128]{1,0:T(8,128)} %bitcast.7), custom_call_target="tpu_custom_call" | custom-call | flops 2147483648 | bytes 1048576 | tf_op jit(solution)/shard_map/pallas_call | solution.py:464
  52.9 0.6 %copy.9 = f32[3,512]{1,0:T(4,128)} copy(f32[3,512]{1,0:T(4,128)S(1)} %shard_map.73) | data formatting | bytes 12288
